TPU v7x, 256 devices: a whole 4x4x8 slice. The times are simulated.
256 devices in a mesh: grp: 32 (over z_hi, y, core), sp: 8 (over x, z_lo).
Axes of the slice: x: 4, y: 4, z: 8 (z_hi: 4, z_lo: 2; z = z_hi * 2 + z_lo), core: 2. Of those that a mesh axis runs over, the one named last changes fastest.
Arguments:
- hidden: bfloat16 [32, 64, 128, 1152], P('grp', 'sp'), may hold values from -60 to 60
- frame_counts: int32 [32], P('grp'), may hold values from 1 to 48, 819 in all
- shifts: float32 [32, 4, 1152], P('grp'), may hold values from -3 to 3
- gates: float32 [32, 2, 1152], P('grp'), may hold values from 0.25 to 1.75
- w_qkv_spatial: bfloat16 [1152, 1728], P('grp'), may hold values from -1 to 1
- w_out_spatial: bfloat16 [576, 1152], P('grp'), may hold values from -0.25 to 0.25
- w_qkv_temporal: bfloat16 [1152, 1728], P('grp'), may hold values from -1 to 1
- w_out_temporal: bfloat16 [576, 1152], P('grp'), may hold values from -0.25 to 0.25
- cotangent: bfloat16 [32, 64, 128, 1152], P('grp', 'sp'), may hold values from -6 to 6
Outputs:
- block_out: bfloat16 [32, 64, 128, 1152], P('grp', 'sp')
- grad_out_temporal: float32 [1152, 576], P('grp', 'sp')
Inputs may be any that keep to these rules, and one draw needn't show every extreme that they name: `frame_counts`: each clip has at least one frame; the longest clip has exactly 48 frames and all clips together have 819.
All inputs are finite; a program needn't handle non-finite values. No bound on the sum of `frame_counts` on one device may be relied on, other than what follows from the above.
Results may differ from a plain program's by a relative error of at most 0.034.
Values may be sent and summed in bfloat16 or wider, within the bound.
A program may use at most 128 MiB of HBM per device.

v0:
```python
import math

import jax
import jax.numpy as jnp
from jax import lax
from jax.sharding import PartitionSpec as P

HDIM = 72
HEADS = 8


def layer_norm(values):
    values = values.astype(jnp.float32)
    centre = jnp.mean(values, axis=-1, keepdims=True)
    centred = values - centre
    spread = jnp.mean(centred * centred, axis=-1, keepdims=True)
    return centred * lax.rsqrt(spread + 1e-06)


def modulate(values, offsets, shift_row, scale_row):
    return (layer_norm(values) * (1.0 + offsets[scale_row]) + offsets[shift_row]).astype(
        jnp.bfloat16
    )


def softmax_rows(scores):
    scores = scores - jnp.max(scores, axis=-1, keepdims=True)
    expo = jnp.exp(scores)
    return (expo / jnp.sum(expo, axis=-1, keepdims=True)).astype(jnp.bfloat16)


def spatial_frame(one_frame, offsets, gating, proj_weight, out_weight):
    pixels = one_frame.shape[0]
    inner = out_weight.shape[0]
    normed = modulate(one_frame, offsets, 0, 1)
    projected = jnp.dot(normed, proj_weight, preferred_element_type=jnp.float32).astype(
        jnp.bfloat16
    )
    projected = projected.reshape(pixels, 3, HEADS, HDIM)
    scores = jnp.einsum(
        "qhd,khd->hqk", projected[:, 0], projected[:, 1], preferred_element_type=jnp.float32
    ) / math.sqrt(HDIM)
    probs = softmax_rows(scores)
    attended = jnp.einsum(
        "hqk,khd->qhd", probs, projected[:, 2], preferred_element_type=jnp.float32
    )
    attended = attended.astype(jnp.bfloat16).reshape(pixels, inner)
    branch = jnp.dot(attended, out_weight, preferred_element_type=jnp.float32)
    return (one_frame.astype(jnp.float32) + gating[0] * branch).astype(jnp.bfloat16)


def spatial_slots(frames, alive_slots, offsets, gating, proj_weight, out_weight):

    def advance(position, finished):
        one_frame = lax.dynamic_index_in_dim(finished, position, 0, keepdims=False)
        result = lax.cond(
            alive_slots[position],
            lambda picked: spatial_frame(picked, offsets, gating, proj_weight, out_weight),
            lambda picked: picked,
            one_frame,
        )
        return lax.dynamic_update_index_in_dim(finished, result, position, 0)

    return lax.fori_loop(0, frames.shape[0], advance, frames)


def frame_mixing(projected, frame_total):
    frames, columns = (projected.shape[0], projected.shape[1])
    split_heads = projected.reshape(frames, columns, 3, HEADS, HDIM)
    scores = jnp.einsum(
        "qphd,kphd->phqk",
        split_heads[:, :, 0],
        split_heads[:, :, 1],
        preferred_element_type=jnp.float32,
    ) / math.sqrt(HDIM)
    allowed = jnp.arange(frames) < frame_total
    scores = jnp.where(allowed[None, None, None, :], scores, -1e30)
    probs = softmax_rows(scores)
    mixed = jnp.einsum(
        "phqk,kphd->qphd", probs, split_heads[:, :, 2], preferred_element_type=jnp.float32
    )
    return mixed.astype(jnp.bfloat16).reshape(frames, columns, HEADS * HDIM)


def on_device(
    hidden,
    frame_counts,
    shifts,
    gates,
    w_qkv_spatial,
    w_out_spatial,
    w_qkv_temporal,
    w_out_temporal,
    cotangent,
):
    sp_rank = lax.axis_index("sp")
    own_frames = hidden[0]
    slots, pixels, width = own_frames.shape
    frame_total = frame_counts[0]
    offsets = shifts[0]
    gating = gates[0]
    slot_ids = jnp.arange(slots, dtype=jnp.int32)
    alive_own = sp_rank * slots + slot_ids < frame_total
    proj_spatial, out_spatial, proj_temporal, out_temporal = (
        lax.all_gather(w_qkv_spatial, "grp", axis=0, tiled=True),
        lax.all_gather(w_out_spatial, "grp", axis=0, tiled=True),
        lax.all_gather(w_qkv_temporal, "grp", axis=0, tiled=True),
        lax.all_gather(w_out_temporal, "grp", axis=0, tiled=True),
    )
    inner = out_spatial.shape[0]
    middle = spatial_slots(own_frames, alive_own, offsets, gating, proj_spatial, out_spatial)
    normed_t = modulate(middle, offsets, 2, 3)
    pixel_rows = lax.all_to_all(normed_t, "sp", split_axis=1, concat_axis=0, tiled=True)
    all_frames, own_pixels = (pixel_rows.shape[0], pixel_rows.shape[1])
    projected_rows = jnp.dot(
        pixel_rows.reshape(all_frames * own_pixels, width),
        proj_temporal,
        preferred_element_type=jnp.float32,
    )
    by_pixel = projected_rows.astype(jnp.bfloat16).reshape(all_frames, own_pixels, 3 * inner)
    mixed = frame_mixing(by_pixel, frame_total)
    attended_t = lax.all_to_all(mixed, "sp", split_axis=0, concat_axis=1, tiled=True)
    flat_attended = attended_t.reshape(slots * pixels, inner)
    branch_t = jnp.dot(flat_attended, out_temporal, preferred_element_type=jnp.float32).reshape(
        slots, pixels, width
    )
    kept_rows = alive_own[:, None, None]
    block_out = jnp.where(kept_rows, middle.astype(jnp.float32) + gating[1] * branch_t, 0.0).astype(
        jnp.bfloat16
    )
    scaled = jnp.where(kept_rows, gating[1] * cotangent[0].astype(jnp.float32), 0.0).astype(
        jnp.bfloat16
    )
    scaled = scaled.reshape(slots * pixels, width)
    whole_grad = (
        lax.dot_general(
            scaled, flat_attended, (((0,), (0,)), ((), ())), preferred_element_type=jnp.float32
        )
        / pixels
    )
    by_columns = lax.psum_scatter(
        whole_grad.astype(jnp.bfloat16), "sp", scatter_dimension=1, tiled=True
    )
    grad_block = lax.psum_scatter(by_columns, "grp", scatter_dimension=0, tiled=True).astype(
        jnp.float32
    )
    return (block_out[None], grad_block)


def solution(mesh):
    return jax.shard_map(
        on_device,
        mesh=mesh,
        in_specs=(
            P("grp", "sp", None, None),
            P("grp"),
            P("grp", None, None),
            P("grp", None, None),
            P("grp", None),
            P("grp", None),
            P("grp", None),
            P("grp", None),
            P("grp", "sp", None, None),
        ),
        out_specs=(P("grp", "sp", None, None), P("grp", "sp")),
        check_vma=False,
    )
```

profile of v0, /device:TPU:7, one launch (start us, length us, event | category | flops | bytes accessed | tf_op | source)
XLA Modules:
  0.0 652.0 jit_solution(7385022359441354244)
XLA Ops:
  10.1 57.3 %all-gather.11.cloned.1.call-done = bf16[32,18,1152]{2,1,0:T(8,128)(2,1)} async-done(((bf16[1,18,1152]{2,1,0:T(8,128)(2,1)}), bf16[32,18,1152]{2,1,0:T(8,128)(2,1)}) %all-gather.11.cloned.1.call-update) | async-done | bytes 1327120 | tf_op jit(solution)/shard_map/all_gather | solution.py:106
  67.4 3.4 reshape.90
  70.9 58.8 %all-gather.9.cloned.1.call-done = bf16[32,36,1728]{2,1,0:T(8,128)(2,1)} async-done(((bf16[1,36,1728]{2,1,0:T(8,128)(2,1)}), bf16[32,36,1728]{2,1,0:T(8,128)(2,1)}) %all-gather.9.cloned.1.call-update) | async-done | bytes 3981328 | tf_op jit(solution)/shard_map/all_gather | solution.py:105
  129.7 7.3 %reshape.88 = bf16[1152,1728]{1,0:T(8,128)(2,1)} reshape(bf16[32,36,1728]{2,1,0:T(8,128)(2,1)} %all-gather.9.cloned.1.call-done) | data formatting | bytes 7962624
  137.0 10.1 %while.13 = (s32[]{:T(128)}, bf16[8,128,1152]{2,1,0:T(8,128)(2,1)S(1)}, pred[8]{0:T(512)(128)(4,1)S(1)}, f32[2,1152]{1,0:T(2,128)S(1)}, f32[4,1152]{1,0:T(4,128)...) while((s32[]{:T(128)}, bf16[8,128,1152]{2,1,0:T(8,128)(2,1)S(1)}, ...), condition=%wide.region_7.8_spmd, body=%wide.region_0.7_spmd.sunk | while | flops 739674624 | bytes 11064472 | solution.py:64
  147.5 0.8 fusion.22
  148.3 0.9 fusion.25
  149.2 2.7 copy.42
  151.9 77.5 %all-to-all-start = ((bf16[8,128,1152]{2,0,1:T(8,128)(2,1)}), bf16[8,128,1152]{2,0,1:T(8,128)(2,1)}, u32[]{:S(2)}, u32[]{:S(2)}) async-start(bf16[8,128,1152]{2,0,1:T(8,128)(2,1)} %copy.42), calls=%async_computation | async-start | bytes 4718592 | tf_op jit(solution)/shard_map/all_to_all | solution.py:113
  230.1 7.3 %reshape.92 = bf16[1152,1728]{1,0:T(8,128)(2,1)} reshape(bf16[32,36,1728]{2,1,0:T(8,128)(2,1)} %all-gather.13.cloned.1.call-done) | data formatting | bytes 7962624
  237.4 22.0 %all-to-all-done = bf16[8,128,1152]{2,0,1:T(8,128)(2,1)} async-done(((bf16[8,128,1152]{2,0,1:T(8,128)(2,1)}), bf16[8,128,1152]{2,0,1:T(8,128)(2,1)}, u32[]{:S(2)}, u32[]{:S(2)}) %all-to-all-start) | async-done | bytes 2359328 | tf_op jit(solution)/shard_map/all_to_all | solution.py:113
  259.4 2.1 copy.44
  262.3 6.3 convolution_convert_fusion.2
  268.6 5.8 copy.45
  274.5 11.2 %reshape_reshape.3 = bf16[64,16,3,8,72]{4,3,2,1,0:T(8,128)(2,1)} reshape(bf16[1024,1728]{1,0:T(8,128)(2,1)} %copy.45) | data formatting | bytes 7077888 | tf_op jit(solution)/shard_map/reshape;reshape | solution.py:69
  285.6 5.5 fusion.40
  291.1 2.5 fusion.32
  293.7 1.7 fusion.41
  295.3 2.5 convert_bitcast_fusion
  297.9 2.7 copy.50
  300.6 4.2 reshape.84
  304.8 5.7 all-to-all-start.1
  310.6 3.8 select_convert_fusion
  314.3 11.6 %all-to-all-done.1 = bf16[64,16,576]{2,1,0:T(8,128)(2,1)} async-done(((bf16[64,16,576]{2,1,0:T(8,128)(2,1)}), bf16[64,16,576]{2,1,0:T(8,128)(2,1)}, u32[]{:S(2)}, u32[]{:S(2)}) %all-to-all-start.1) | async-done | bytes 1179680 | tf_op jit(solution)/shard_map/all_to_all | solution.py:122
  326.0 1.6 copy.51
  327.6 1.1 copy-done.3
  328.7 2.9 fusion.30
  332.9 3.5 reshape.95
  336.3 33.8 %reduce-scatter.6.cloned.1.call-done = bf16[1152,72]{0,1:T(8,128)(2,1)} async-done(((bf16[1152,576]{0,1:T(8,128)(2,1)}), bf16[1152,72]{0,1:T(8,128)(2,1)}) %reduce-scatter.6.cloned.1.call-update) | async-done | bytes 165904
  370.1 5.2 fusion.28
  375.4 268.2 %all-reduce.4.cloned.1.call-done = bf16[1152,72]{0,1:T(8,128)(2,1)} async-done(((bf16[1152,72]{0,1:T(8,128)(2,1)}), bf16[1152,72]{0,1:T(8,128)(2,1)}) %all-reduce.4.cloned.1.call-update) | async-done | bytes 165904
  643.6 0.8 dynamic-slice_convert_fusion
  (68 shorter events, 10.6 us)
Async XLA Ops:
  7.2 2.9 copy-start.4
  7.2 60.2 %all-gather.11.cloned.1.call-start = ((), (), s32[]{:S(2)}) async-start(), calls=%async_computation.4 | async-start | bytes 1824768 | tf_op jit(solution)/shard_map/all_gather | solution.py:106
  7.9 121.8 %all-gather.9.cloned.1.call-start = ((), (), s32[]{:S(2)}) async-start(), calls=%async_computation.3 | async-start | bytes 4730880 | tf_op jit(solution)/shard_map/all_gather | solution.py:105
  8.7 221.4 %all-gather.13.cloned.1.call-start = ((), (), s32[]{:S(2)}) async-start(), calls=%async_computation.5 | async-start | bytes 4730880 | tf_op jit(solution)/shard_map/all_gather | solution.py:107
  70.9 66.1 %copy-start = (bf16[1,8,128,1152]{3,2,1,0:T(8,128)(2,1)S(1)}, bf16[1,8,128,1152]{3,2,1,0:T(8,128)(2,1)}, u32[]{:S(2)}) copy-start(bf16[1,8,128,1152]{3,2,1,0:T(8,128)(2,1)} %param.13) | copy-start | bytes 7077892
  70.9 66.1 %copy-start.5 = (f32[1,2,1152]{2,1,0:T(2,128)S(1)}, f32[1,2,1152]{2,1,0:T(2,128)}, u32[]{:S(2)}) copy-start(f32[1,2,1152]{2,1,0:T(2,128)} %param.16) | copy-start | bytes 27652
  151.9 107.5 %all-to-all-start = ((bf16[8,128,1152]{2,0,1:T(8,128)(2,1)}), bf16[8,128,1152]{2,0,1:T(8,128)(2,1)}, u32[]{:S(2)}, u32[]{:S(2)}) async-start(bf16[8,128,1152]{2,0,1:T(8,128)(2,1)} %copy.42), calls=%async_computation | async-start | bytes 4718592 | tf_op jit(solution)/shard_map/all_to_all | solution.py:113
  229.5 103.4 %all-gather.15.cloned.1.call-start = ((), (), s32[]{:S(2)}) async-start(), calls=%async_computation.6 | async-start | bytes 1824768 | tf_op jit(solution)/shard_map/all_gather | solution.py:108
  259.4 2.9 copy-start.1
  304.8 21.2 %all-to-all-start.1 = ((bf16[64,16,576]{2,1,0:T(8,128)(2,1)}), bf16[64,16,576]{2,1,0:T(8,128)(2,1)}, u32[]{:S(2)}, u32[]{:S(2)}) async-start(bf16[64,16,576]{2,1,0:T(8,128)(2,1)} %reshape.84), calls=%async_computation.1 | async-start | bytes 2621440 | tf_op jit(solution)/shard_map/all_to_all | solution.py:122
  310.5 59.6 %reduce-scatter.6.cloned.1.call-start = ((), (), s32[]{:S(2)}) async-start(), calls=%async_computation.8 | async-start | bytes 1492992
  326.0 2.7 copy-start.2
  327.6 1.1 copy-start.3
  328.7 2.9 copy-start.6
  331.5 312.0 %all-reduce.4.cloned.1.call-start = ((), (), s32[]{:S(2)}) async-start(), calls=%async_computation.7 | async-start | bytes 331776
Sparse Core Ops, SparseCore 0:
  10.6 56.8 all-gather.10
  70.0 59.6 all-gather.8
  132.3 60.0 all-gather.12
  232.5 51.7 all-gather.14
  331.7 38.4 reduce-scatter.5
  372.8 270.7 all-reduce.3
where the time goes:
time: 656 us; the launch traced here: 652 us
  waiting for transfers between devices  454 us (69%)
  starting transfers between devices  83.4 us (13%)
  local copies, waits for them, and re-layouts  65.7 us (10%)
  matrix products  19.5 us (3%)
  between operations  15.5 us (2%)
  other arithmetic  8.43 us (1%)
    unnamed x8, waiting for transfers between devices  305 us
    all_to_all x1, starting transfers between devices, on_device(): lax.all_to_all(normed_t, 'sp', split_axis=1, concat_axis=0, tiled=True)  77.5 us
    all_gather x1, waiting for transfers between devices, on_device(): lax.all_gather(w_qkv_spatial, 'grp', axis=0, tiled=True)  58.8 us
    all_gather x1, waiting for transfers between devices, on_device(): lax.all_gather(w_out_spatial, 'grp', axis=0, tiled=True)  57.3 us
    unnamed x20, local copies, waits for them, and re-layouts  24.6 us
    all_to_all x1, waiting for transfers between devices, on_device(): lax.all_to_all(normed_t, 'sp', split_axis=1, concat_axis=0, tiled=True)  22 us
  transfers between devices with their start and end apart: 8, of which 6 were waited for; matrix products, arithmetic and copies ran while one was open for 14% of the time, Pallas kernels for 0%

commit v1 on v0

v1 whole, which is shorter than its diff:
```python
import functools
import math

import jax
import jax.numpy as jnp
from jax import lax
from jax.experimental import pallas as pl
from jax.experimental.pallas import tpu as pltpu
from jax.sharding import PartitionSpec as P

MESH = pl.DeviceIdType.MESH
BF = jnp.bfloat16
F32 = jnp.float32
HDIM = 72
WIDTH = 1152
INNER = 576
PAD = 640
PIX = 128
SLOTS = 8
OWN = 16
SENDERS = 6
PACK = 1792
SCALE = math.log2(math.e) / math.sqrt(HDIM)
ANY = pl.BlockSpec(memory_space=pl.ANY)
VM = pl.BlockSpec(memory_space=pltpu.VMEM)
SM = pl.BlockSpec(memory_space=pltpu.SMEM)
BIG = 56 * 1024 * 1024


def params(cid=None):
    if cid is None:
        return pltpu.CompilerParams(vmem_limit_bytes=BIG)
    return pltpu.CompilerParams(vmem_limit_bytes=BIG, collective_id=cid, has_side_effects=True)


def greet(partners):
    barrier = pltpu.get_barrier_semaphore()
    for who in partners:
        pl.semaphore_signal(barrier, inc=1, device_id=who, device_id_type=MESH)
    pl.semaphore_wait(barrier, len(partners))


def gather_kernel(own_ref, full, ssem, rsem, lsem):
    grp, sp = lax.axis_index("grp"), lax.axis_index("sp")
    h, y, c = grp // 8, (grp // 2) % 4, grp % 2
    low = sp % 2
    up, down, far = lax.rem(y + 1, 4), lax.rem(y + 3, 4), lax.rem(y + 2, 4)
    hx = lax.rem(h + 3 + 2 * low, 4)
    hp = lax.rem(h + 5 - 2 * low, 4)
    hf = lax.rem(h + 2, 4)
    sibling = (grp + 1 - 2 * c, sp)
    y_up = ((h * 4 + up) * 2 + c, sp)
    y_down = ((h * 4 + down) * 2 + c, sp)
    pair = (grp, sp + 1 - 2 * low)
    cross = (hx * 8 + y * 2 + c, sp + 1 - 2 * low)
    half = PACK
    cols_mine = pl.ds(pl.multiple_of(c * half, 128), half)
    cols_other = pl.ds(pl.multiple_of((1 - c) * half, 128), half)
    ca = pl.ds(pl.multiple_of(c * half, 128), half // 2)
    cb = pl.ds(pl.multiple_of(c * half + half // 2, 128), half // 2)

    local = pltpu.make_async_copy(own_ref.at[:, cols_mine], full.at[h, y, c, :, cols_mine], lsem)
    local.start()
    greet([sibling, y_up, y_down, pair, cross])
    count = [0]

    def send(src, dst, who):
        i = count[0]
        count[0] += 1
        copy = pltpu.make_async_remote_copy(
            src_ref=src, dst_ref=dst, send_sem=ssem.at[i], recv_sem=rsem.at[i],
            device_id=who, device_id_type=MESH)
        copy.start()
        return copy

    everything = []

    def go(where, who):
        part = full.at[where]
        copy = send(part, part, who)
        everything.append(copy)
        return copy

    al = slice(None)
    first = send(own_ref.at[:, cols_other], full.at[h, y, c, :, cols_other], sibling)
    local.wait()
    first.wait()
    by1 = [go((h, y, al, al, cb), y_up), go((h, y, al, al, cb), y_down)]
    az1 = go((h, y, al, al, ca), cross)
    for copy in by1:
        copy.wait_recv()
    by2 = [go((h, down, 0, al, cb), y_up), go((h, up, 1, al, cb), y_down)]
    az1.wait_recv()
    az2 = go((hx, y, al, al, ca), pair)
    for copy in by2:
        copy.wait_recv()
    bz1 = go((h, al, al, al, cb), cross)
    last = [go((h, al, al, al, cb), sibling)]
    az2.wait_recv()
    az3 = go((hp, y, 1 - low, al, ca), cross)
    az3.wait_recv()
    az4 = go((hf, y, low, al, ca), pair)
    az4.wait_recv()
    ay1 = [go((al, y, al, al, ca), y_up), go((al, y, al, al, ca), y_down)]
    last.append(go((al, y, al, al, ca), sibling))
    bz1.wait_recv()
    bz2 = go((hx, al, al, al, cb), pair)
    last.append(go((hx, al, al, al, cb), sibling))
    for copy in ay1:
        copy.wait_recv()
    ay2 = [go((al, down, 0, al, ca), y_up), go((al, up, 1, al, ca), y_down)]
    last.append(go((al, down, al, al, ca), sibling))
    last.append(go((al, up, al, al, ca), sibling))
    bz2.wait_recv()
    bz3 = go((hp, al, 1 - low, al, cb), cross)
    last.append(go((hp, al, al, al, cb), sibling))
    bz3.wait_recv()
    bz4 = go((hf, al, low, al, cb), pair)
    for copy in ay2:
        copy.wait_recv()
    last.append(go((al, far, al, al, ca), sibling))
    bz4.wait_recv()
    last.append(go((hf, al, al, al, cb), sibling))
    for copy in last:
        copy.wait_recv()
    for copy in everything:
        copy.wait_send()


GATHER_COPIES = 25


def gather(own):
    rows, columns = own.shape
    return pl.pallas_call(
        gather_kernel,
        out_shape=jax.ShapeDtypeStruct((4, 4, 2, rows, columns), BF),
        in_specs=[ANY],
        out_specs=ANY,
        scratch_shapes=[
            pltpu.SemaphoreType.DMA((GATHER_COPIES,)),
            pltpu.SemaphoreType.DMA((GATHER_COPIES,)),
            pltpu.SemaphoreType.DMA,
        ],
        compiler_params=params(1),
        name="gather",
    )(own)


def pack(qkv, out):
    part = jnp.concatenate([qkv, out.reshape(12, 1728)], axis=0)
    return jnp.pad(part, ((0, 0), (0, PACK - 1728)))


def unpack(part):
    part = part.reshape(32, 48, -1)[:, :, :1728]
    qkv = part[:, :36].reshape(WIDTH, 3, INNER)
    qkv = jnp.pad(qkv, ((0, 0), (0, 0), (0, PAD - INNER))).reshape(WIDTH, 3 * PAD)
    out = jnp.pad(part[:, 36:].reshape(INNER, WIDTH), ((0, PAD - INNER), (0, 0)))
    return qkv, out


def modulated(x, offsets, shift_row, scale_row):
    mean = jnp.sum(x, axis=-1, keepdims=True) * (1.0 / WIDTH)
    x = x - mean
    spread = jnp.sum(x * x, axis=-1, keepdims=True) * (1.0 / WIDTH)
    x = x * lax.rsqrt(spread + 1e-06)
    return (x * (1.0 + offsets[scale_row]) + offsets[shift_row]).astype(BF)


def head_masks(j):
    lane = lax.broadcasted_iota(jnp.int32, (1, 256), 1)
    start = 16 * j
    one = ((lane >= start) & (lane < start + HDIM)).astype(F32).astype(BF)
    two = ((lane >= start + HDIM) & (lane < start + 2 * HDIM)).astype(F32).astype(BF)
    return one, two


def attention(load, keys, valid):
    blocks = [None] * 5
    fill = [] if keys == PIX else [jnp.zeros((PIX - keys, 256), BF)]
    for j in range(4):
        one, two = head_masks(j)
        q, k, v = (load(part * PAD + 128 * j) for part in range(3))
        kk = jnp.concatenate([k * one, *fill, k * two, *fill], axis=0)
        vv = jnp.concatenate([v * one, *fill, v * two, *fill], axis=0)
        s = lax.dot_general(q, kk, (((1,), (1,)), ((), ())), preferred_element_type=F32)
        probs = []
        for part in (s[:, :128], s[:, 128:]):
            if valid is not None:
                part = jnp.where(valid, part, -1e30)
            top = jnp.max(part, axis=-1, keepdims=True)
            e = jnp.exp2((part - top) * SCALE)
            probs.append((e * (1.0 / jnp.sum(e, axis=-1, keepdims=True))).astype(BF))
        o = jnp.dot(jnp.concatenate(probs, axis=1), vv, preferred_element_type=F32)
        for i, piece in ((j, o[:, :128]), (j + 1, o[:, 128:])):
            blocks[i] = piece if blocks[i] is None else blocks[i] + piece
    return jnp.concatenate(blocks, axis=1).astype(BF)


def spatial_kernel(x_ref, shift_ref, gate_ref, wq_ref, wo_ref, mid_ref, nt_ref, normed, qkv, att):
    offsets = [shift_ref[i : i + 1, :] for i in range(4)]
    gate = gate_ref[0:1, :]

    @pl.when(lax.axis_index("sp") < SENDERS)
    def _():
        @pl.loop(0, SLOTS)
        def _(f):
            normed[f] = modulated(x_ref[f].astype(F32), offsets, 0, 1)

        @pl.loop(0, 5)
        def _(n):
            cols = pl.ds(pl.multiple_of(n * 384, 128), 384)
            got = jnp.dot(normed[...].reshape(SLOTS * PIX, WIDTH), wq_ref[:, cols], preferred_element_type=F32)
            qkv[:, :, cols] = got.astype(BF).reshape(SLOTS, PIX, 384)

        @pl.loop(0, SLOTS)
        def _(f):
            att[f] = attention(lambda first: qkv[f, :, first : first + 256], PIX, None)

        @pl.loop(0, SLOTS)
        def _(f):
            branch = jnp.dot(att[f], wo_ref[...], preferred_element_type=F32)
            middle = (x_ref[f].astype(F32) + gate * branch).astype(BF)
            mid_ref[f] = middle
            nt_ref[f] = modulated(middle.astype(F32), offsets, 2, 3)


def spatial(hidden, shifts, gates, wq, wo):
    shape = jax.ShapeDtypeStruct((SLOTS, PIX, WIDTH), BF)
    return pl.pallas_call(
        spatial_kernel,
        out_shape=(shape, shape),
        in_specs=[VM] * 5,
        out_specs=(VM, VM),
        scratch_shapes=[
            pltpu.VMEM((SLOTS, PIX, WIDTH), BF),
            pltpu.VMEM((SLOTS, PIX, 3 * PAD), BF),
            pltpu.VMEM((SLOTS, PIX, PAD), BF),
        ],
        compiler_params=params(),
        name="spatial",
    )(hidden, shifts, gates, wq, wo)


def iota(shape, dim):
    return lax.broadcasted_iota(jnp.int32, shape, dim)


def shuffle(back):
    there, here = iota((128, 128), 1 if back else 0), iota((128, 128), 0 if back else 1)
    return (here == (there % 8) * OWN + there // 8).astype(F32).astype(BF)


def temporal_kernel(total_ref, x_ref, wq_ref, out_ref, xp, qkv, ap):
    rows = SENDERS * 16
    there = shuffle(False)
    back = shuffle(True)
    total = total_ref[0]

    @pl.loop(0, SENDERS)
    def _(s):
        got = jnp.dot(there, x_ref[s].reshape(128, WIDTH), preferred_element_type=F32).astype(BF)
        xp[:, s] = got.reshape(8, 16, WIDTH)

    @pl.loop(0, 5)
    def _(n):
        cols = pl.ds(pl.multiple_of(n * 384, 128), 384)
        got = jnp.dot(xp[...].reshape(8 * rows, WIDTH), wq_ref[:, cols], preferred_element_type=F32)
        qkv[:, :, cols] = got.astype(BF).reshape(8, rows, 384)

    key, row = iota((rows, PIX), 1), iota((rows, PIX), 0)
    frame = (key // 16) * 8 + key % 8
    valid = (key < rows) & (frame < total) & ((key // 8) % 2 == (row // 8) % 2)

    @pl.loop(0, 8)
    def _(g):
        got = attention(lambda first: qkv[g, :, first : first + 256], rows, valid)
        ap[:, g] = got.reshape(SENDERS, 16, PAD)

    @pl.loop(0, SENDERS)
    def _(s):
        got = jnp.dot(back, ap[s].reshape(128, PAD), preferred_element_type=F32).astype(BF)
        out_ref[s] = got.reshape(SLOTS, OWN, PAD)


def temporal(total, tokens, wq):
    return pl.pallas_call(
        temporal_kernel,
        out_shape=jax.ShapeDtypeStruct((SENDERS, SLOTS, OWN, PAD), BF),
        in_specs=[SM, VM, VM],
        out_specs=VM,
        scratch_shapes=[
            pltpu.VMEM((8, SENDERS, 16, WIDTH), BF),
            pltpu.VMEM((8, SENDERS * 16, 3 * PAD), BF),
            pltpu.VMEM((SENDERS, 8, 16, PAD), BF),
        ],
        compiler_params=params(),
        name="temporal",
    )(total, tokens, wq)


def finish_kernel(total_ref, att_ref, mid_ref, cot_ref, gate_ref, wo_ref, out_ref, grad_ref, scaled):
    sp = lax.axis_index("sp")
    gate = gate_ref[1:2, :]
    total = total_ref[0]

    @pl.when(sp < SENDERS)
    def _():
        @pl.loop(0, SLOTS)
        def _(f):
            kept = sp * SLOTS + f < total
            branch = jnp.dot(att_ref[f], wo_ref[...], preferred_element_type=F32)
            out = mid_ref[f].astype(F32) + gate * branch
            out_ref[f] = jnp.where(kept, out, 0.0).astype(BF)
            scaled[f] = jnp.where(kept, gate * cot_ref[f].astype(F32), 0.0).astype(BF)

        @pl.loop(0, 3)
        def _(n):
            cols = pl.ds(pl.multiple_of(n * 384, 128), 384)
            got = lax.dot_general(
                att_ref[...].reshape(SLOTS * PIX, PAD), scaled[:, :, cols].reshape(SLOTS * PIX, 384),
                (((0,), (0,)), ((), ())), preferred_element_type=F32) * (1.0 / PIX)
            for t in range(8):
                rows = jnp.concatenate([got[72 * t : 72 * t + 72], jnp.zeros((8, 384), F32)], axis=0)
                grad_ref[t, :, cols] = rows.astype(BF)

    @pl.when(sp >= SENDERS)
    def _():
        out_ref[...] = jnp.zeros_like(out_ref)
        grad_ref[...] = jnp.zeros_like(grad_ref)


def finish(total, att, middle, cotangent, gates, wo):
    return pl.pallas_call(
        finish_kernel,
        out_shape=(
            jax.ShapeDtypeStruct((SLOTS, PIX, WIDTH), BF),
            jax.ShapeDtypeStruct((8, 80, WIDTH), BF),
        ),
        in_specs=[SM] + [VM] * 5,
        out_specs=(VM, VM),
        scratch_shapes=[pltpu.VMEM((SLOTS, PIX, WIDTH), BF)],
        compiler_params=params(),
        name="finish",
    )(total, att, middle, cotangent, gates, wo)


def tokens_there_kernel(nt_ref, x_ref, ssem, rsem, lsem):
    grp, sp = lax.axis_index("grp"), lax.axis_index("sp")
    peers = [(grp, lax.rem(sp + d, 8)) for d in range(1, 8)]
    greet(peers)

    def copy_to(d):
        to = lax.rem(sp + d, 8)
        src = nt_ref.at[:, pl.ds(pl.multiple_of(to * OWN, OWN), OWN), :]
        return pltpu.make_async_remote_copy(
            src_ref=src, dst_ref=x_ref.at[lax.rem(sp, SENDERS)], send_sem=ssem.at[d], recv_sem=rsem.at[d],
            device_id=(grp, to), device_id_type=MESH)

    @pl.when(sp < SENDERS)
    def _():
        for d in (4, 3, 5, 2, 6, 1, 7):
            copy_to(d).start()
        mine = pltpu.make_async_copy(
            nt_ref.at[:, pl.ds(pl.multiple_of(sp * OWN, OWN), OWN), :], x_ref.at[lax.rem(sp, SENDERS)], lsem)
        mine.start()
        mine.wait()
        for d in range(1, 8):
            copy_to(d).wait_send()

    for d in range(1, 8):
        @pl.when(lax.rem(sp + 8 - d, 8) < SENDERS)
        def _(d=d):
            copy_to(d).wait_recv()


def tokens_back_kernel(a_ref, att_ref, ssem, rsem, lsem):
    grp, sp = lax.axis_index("grp"), lax.axis_index("sp")
    peers = [(grp, lax.rem(sp + d, 8)) for d in range(1, 8)]
    greet(peers)
    mine = att_ref.at[:, pl.ds(pl.multiple_of(sp * OWN, OWN), OWN), :]

    def copy_to(d):
        to = lax.rem(sp + d, 8)
        return pltpu.make_async_remote_copy(
            src_ref=a_ref.at[lax.rem(to, SENDERS)], dst_ref=mine, send_sem=ssem.at[d], recv_sem=rsem.at[d],
            device_id=(grp, to), device_id_type=MESH)

    for d in (4, 3, 5, 2, 6, 1, 7):
        @pl.when(lax.rem(sp + d, 8) < SENDERS)
        def _(d=d):
            copy_to(d).start()

    @pl.when(sp < SENDERS)
    def _():
        own = pltpu.make_async_copy(a_ref.at[lax.rem(sp, SENDERS)], mine, lsem)
        own.start()
        own.wait()
        for d in range(1, 8):
            copy_to(d).wait_recv()

    for d in range(1, 8):
        @pl.when(lax.rem(sp + d, 8) < SENDERS)
        def _(d=d):
            copy_to(d).wait_send()


def exchange(kernel, cid, name, shape, array):
    return pl.pallas_call(
        kernel,
        out_shape=jax.ShapeDtypeStruct(shape, BF),
        in_specs=[ANY],
        out_specs=ANY,
        scratch_shapes=[
            pltpu.SemaphoreType.DMA((8,)),
            pltpu.SemaphoreType.DMA((8,)),
            pltpu.SemaphoreType.DMA,
        ],
        compiler_params=params(cid),
        name=name,
    )(array)


def reduce_kernel(g_ref, out_ref, r0, red, r1, flipped, buf, r2, s0, t0, s1, t1, s2, t2):
    grp, sp = lax.axis_index("grp"), lax.axis_index("sp")
    c, low, x = grp % 2, sp % 2, sp // 2
    chip = grp // 2
    sibling = (grp + 1 - 2 * c, sp)
    greet([(lax.rem(grp + d, 32), sp) for d in range(1, 32)] + [(grp, lax.rem(sp + d, 8)) for d in range(1, 8)])

    swap = pltpu.make_async_remote_copy(
        src_ref=g_ref.at[:, 1 - c], dst_ref=r0, send_sem=s0, recv_sem=t0, device_id=sibling, device_id_type=MESH)
    swap.start()
    swap.wait()

    slot = lax.rem(sp, SENDERS)

    def step1(to_x):
        return pltpu.make_async_remote_copy(
            src_ref=red.at[to_x], dst_ref=r1.at[slot], send_sem=s1.at[to_x], recv_sem=t1.at[slot],
            device_id=(grp, 2 * to_x + c), device_id_type=MESH)

    @pl.when(sp < SENDERS)
    def _():
        for i in range(4):
            red[i] = (g_ref[i, c].astype(F32) + r0[i].astype(F32)).astype(BF)
        for i in range(4):
            @pl.when(2 * i + c != sp)
            def _(i=i):
                step1(i).start()

            @pl.when(2 * i + c == sp)
            def _(i=i):
                r1[slot] = red[i]

        for i in range(4):
            @pl.when(2 * i + c != sp)
            def _(i=i):
                step1(i).wait_send()

    def step2(d):
        to = lax.rem(grp + d, 32)
        return pltpu.make_async_remote_copy(
            src_ref=buf.at[to], dst_ref=r2.at[chip], send_sem=s2.at[d], recv_sem=t2.at[d],
            device_id=(to, sp), device_id_type=MESH)

    @pl.when(low == c)
    def _():
        for s in range(SENDERS):
            @pl.when(sp != s)
            def _(s=s):
                pltpu.make_async_remote_copy(
                    src_ref=red.at[0], dst_ref=r1.at[s], send_sem=s1.at[0], recv_sem=t1.at[s],
                    device_id=sibling, device_id_type=MESH).wait_recv()

        total = r1[0].astype(F32)
        for s in range(1, SENDERS):
            total = total + r1[s].astype(F32)
        total = jnp.concatenate([total, jnp.zeros((48, WIDTH), F32)], axis=0)
        for n in range(9):
            flipped[128 * n : 128 * n + 128] = total[:, 128 * n : 128 * n + 128].T
        for g in range(32):
            rows = jnp.concatenate([flipped[36 * g : 36 * g + 36], jnp.zeros((12, 128), F32)], axis=0)
            buf[g] = rows.astype(BF)

        @pl.loop(1, 32)
        def _(d):
            step2(d).start()

        r2[chip] = buf[grp]

        @pl.loop(1, 32)
        def _(d):
            step2(d).wait_send()

    @pl.loop(1, 32)
    def _(d):
        @pl.when(lax.rem(grp + 32 - d, 2) == low)
        def _():
            step2(d).wait_recv()

    total = r2[0].astype(F32)
    for i in range(1, 16):
        total = total + r2[i].astype(F32)
    out_ref[...] = total


def reduce_gradient(parts):
    return pl.pallas_call(
        reduce_kernel,
        out_shape=jax.ShapeDtypeStruct((48, 128), F32),
        in_specs=[VM],
        out_specs=VM,
        scratch_shapes=[
            pltpu.VMEM((4, 80, WIDTH), BF),
            pltpu.VMEM((4, 80, WIDTH), BF),
            pltpu.VMEM((SENDERS, 80, WIDTH), BF),
            pltpu.VMEM((WIDTH, 128), F32),
            pltpu.VMEM((32, 48, 128), BF),
            pltpu.VMEM((16, 48, 128), BF),
            pltpu.SemaphoreType.DMA,
            pltpu.SemaphoreType.DMA,
            pltpu.SemaphoreType.DMA((4,)),
            pltpu.SemaphoreType.DMA((SENDERS,)),
            pltpu.SemaphoreType.DMA((32,)),
            pltpu.SemaphoreType.DMA((32,)),
        ],
        compiler_params=params(4),
        name="reduce_gradient",
    )(parts)


def on_device(
    hidden,
    frame_counts,
    shifts,
    gates,
    w_qkv_spatial,
    w_out_spatial,
    w_qkv_temporal,
    w_out_temporal,
    cotangent,
):
    own = jnp.concatenate(
        [pack(w_qkv_spatial, w_out_spatial), pack(w_qkv_temporal, w_out_temporal)], axis=1
    )
    full = gather(own)
    wq_s, wo_s = unpack(full[..., :PACK])
    wq_t, wo_t = unpack(full[..., PACK:])
    middle, normed_t = spatial(hidden[0], shifts[0], gates[0], wq_s, wo_s)
    tokens = exchange(tokens_there_kernel, 2, "tokens_there", (SENDERS, SLOTS, OWN, WIDTH), normed_t)
    mixed = temporal(frame_counts, tokens, wq_t)
    att = exchange(tokens_back_kernel, 3, "tokens_back", (SLOTS, PIX, PAD), mixed)
    block_out, parts = finish(frame_counts, att, middle, cotangent[0], gates[0], wo_t)
    grad = reduce_gradient(parts.reshape(4, 2, 80, WIDTH))
    return block_out[None], grad[:36, :HDIM]


def solution(mesh):
    return jax.shard_map(
        on_device,
        mesh=mesh,
        in_specs=(
            P("grp", "sp", None, None),
            P("grp"),
            P("grp", None, None),
            P("grp", None, None),
            P("grp", None),
            P("grp", None),
            P("grp", None),
            P("grp", None),
            P("grp", "sp", None, None),
        ),
        out_specs=(P("grp", "sp", None, None), P("grp", "sp")),
        check_vma=False,
    )
```

time: 656 us -> 331 us (0.50)
  waiting for transfers between devices: 454 us -> 0 us
  Pallas kernels: 0 us -> 229 us
  starting transfers between devices: 83.4 us -> 0 us
  local copies, waits for them, and re-layouts: 65.7 us -> 97.1 us
  matrix products: 19.5 us -> 0 us
  between operations: 15.5 us -> 1.38 us
  other arithmetic: 8.43 us -> 1.79 us
    unnamed x8 -> x0, waiting for transfers between devices: 305 us -> none
    pallas_call x0 -> x7, Pallas kernels: none -> 229 us  [the longest x1 77.7 us: gather(): pl.pallas_call(gather_kernel, out_shape=jax.ShapeDtypeStruct((4, 4, 2, ro...]
    all_gather x4 -> x0, waiting for transfers between devices: 116 us -> none  [the longest x1 58.8 us: on_device(): lax.all_gather(w_qkv_spatial, 'grp', axis=0, tiled=True)]
    all_to_all x2 -> x0, starting transfers between devices: 83.3 us -> none  [the longest x1 77.5 us: on_device(): lax.all_to_all(normed_t, 'sp', split_axis=1, concat_axis=0, tiled=True)]
    reshape x1 -> x8, local copies, waits for them, and re-layouts: 4.24 us -> 41.3 us  [the longest x2 21.7 us: unpack(): qkv = part[:, :36].reshape(WIDTH, 3, INNER)]
    all_to_all x2 -> x0, waiting for transfers between devices: 33.7 us -> none  [the longest x1 22 us: on_device(): lax.all_to_all(normed_t, 'sp', split_axis=1, concat_axis=0, tiled=True)]
    dot_general x5 -> x0, matrix products: 19.5 us -> none  [the longest x1 6.33 us: on_device(): jnp.dot(pixel_rows.reshape(all_frames * own_pixels, width), proj_temporal...]
    slice x2 -> x6, local copies, waits for them, and re-layouts: 5.51 us -> 21.5 us  [the longest x1 9.13 us: on_device(): wq_t, wo_t = unpack(full[..., PACK:])]
  transfers between devices with their start and end apart: 8 -> 0, of which waited for: 6 -> 0; matrix products, arithmetic and copies ran while one was open for 14% -> 0% of each run, Pallas kernels for 0% -> 0%
where the time goes in v1:
time: 331 us; the launch traced here: 329 us
  Pallas kernels  229 us (69%)
  local copies, waits for them, and re-layouts  97.1 us (29%)
    pallas_call x1, Pallas kernels, gather(): pl.pallas_call(gather_kernel, out_shape=jax.ShapeDtypeStruct((4, 4, 2, ro...  77.7 us
    pallas_call x2, Pallas kernels, exchange(): pl.pallas_call(kernel, out_shape=jax.ShapeDtypeStruct(shape, BF), in_spec...  74.8 us
    pallas_call x1, Pallas kernels, reduce_gradient(): pl.pallas_call(reduce_kernel, out_shape=jax.ShapeDtypeStruct((48, 128), F...  39.8 us
    pallas_call x1, Pallas kernels, temporal(): pl.pallas_call(temporal_kernel, out_shape=jax.ShapeDtypeStruct((SENDERS,...  24.9 us
    unnamed x6, local copies, waits for them, and re-layouts  22.7 us
    reshape x2, local copies, waits for them, and re-layouts, unpack(): qkv = part[:, :36].reshape(WIDTH, 3, INNER)  21.7 us
    reshape x2, local copies, waits for them, and re-layouts, unpack(): jnp.pad(qkv, ((0, 0), (0, 0), (0, PAD - INNER))).reshape(WIDTH, 3 * PAD)  13.3 us
    slice x1, local copies, waits for them, and re-layouts, on_device(): wq_t, wo_t = unpack(full[..., PACK:])  9.13 us

profile of v1, /device:TPU:7, one launch (start us, length us, event | category | flops | bytes accessed | tf_op | source)
XLA Modules:
  0.0 328.9 jit_solution(11310815779768901330)
XLA Ops:
  0.6 0.9 reshape.37
  1.6 0.9 reshape.38
  2.5 1.0 fusion.4
  3.5 0.8 pad_maximum_fusion.own_ref
  4.3 77.7 %gather.1 = bf16[4,4,2,48,3584]{4,3,2,1,0:T(8,128)(2,1)} custom-call(bf16[48,3584]{1,0:T(8,128)(2,1)} %pad_maximum_fusion.own_ref), custom_call_target="tpu_custom_call" | custom-call | tf_op jit(solution)/shard_map/gather/pallas_call | solution.py:135
  82.0 9.1 %fusion.6 = (bf16[4,4,2,48,1792]{4,3,2,1,0:T(8,128)(2,1)}, bf16[4,4,2,48,1792]{4,3,2,1,0:T(8,128)(2,1)}) fusion(bf16[4,4,2,48,3584]{4,3,2,1,0:T(8,128)(2,1)} %gather.1), kind=kLoop, calls=%fused_computation.8 | loop fusion | bytes 22020096 | tf_op jit(solution)/shard_map/slice | solution.py:550
  91.1 4.7 %slice.34 = bf16[32,36,1728]{2,1,0:T(8,128)(2,1)} slice(bf16[32,48,1792]{2,1,0:T(8,128)(2,1)} %bitcast.14), slice={[0:32], [0:36], [0:1728]} | slice | bytes 7962624 | tf_op jit(solution)/shard_map/slice | solution.py:157
  95.8 10.8 %reshape.40 = bf16[1152,3,576]{2,1,0:T(4,128)(2,1)} reshape(bf16[32,36,1728]{2,1,0:T(8,128)(2,1)} %slice.34) | data formatting | bytes 7962624 | tf_op jit(solution)/shard_map/reshape | solution.py:157
  106.6 11.3 %copy.15 = bf16[1152,3,576]{0,2,1:T(8,128)(2,1)} copy(bf16[1152,3,576]{2,1,0:T(4,128)(2,1)} %reshape.40) | data formatting | bytes 7962624
  118.0 4.5 %pad.23.clone = bf16[1152,3,640]{0,2,1:T(8,128)(2,1)} pad(bf16[1152,3,576]{0,2,1:T(8,128)(2,1)} %copy.15, bf16[]{:T(256)} %constant.2.clone.1), padding=0_0x0_0x0_64 | pad | bytes 8404994 | tf_op jit(solution)/shard_map/jit(_pad)/pad | solution.py:158
  122.4 6.7 %copy.12.wq_ref = bf16[1152,1920]{1,0:T(8,128)(2,1)} copy(bf16[1152,1920]{0,1:T(8,128)(2,1)} %bitcast.16) | data formatting | bytes 8847360 | tf_op jit(solution)/shard_map/reshape | solution.py:158
  129.1 2.0 slice.35
  131.1 2.2 reshape.42
  133.3 0.0 slice-start
  133.4 1.3 pad.24.wo_ref
  134.7 6.1 %spatial.1 = (bf16[8,128,1152]{2,1,0:T(8,128)(2,1)}, bf16[8,128,1152]{2,1,0:T(8,128)(2,1)}) custom-call(bf16[8,128,1152]{2,1,0:T(8,128)(2,1)} %bitcast.19, f32[4,1152]{1,0:T(4,128)} %bitcast.23, f32[2,1152]{1,0:T(2,128)} %bitcast.21, bf16[1152,1920]{1,0:T(8,128)(2,1)} %copy.12.wq_ref, bf16[640,1152]{1,0:T(8,128)(2,1)} %pad.24.wo_ref), custom_call_target="tpu_custom_call" | custom-call | tf_op jit(solution)/shard_map/spatial/pallas_call | solution.py:231
  140.7 58.0 %tokens_there.1.x_ref = bf16[6,8,16,1152]{3,2,1,0:T(8,128)(2,1)} custom-call(bf16[8,128,1152]{2,1,0:T(8,128)(2,1)} %get-tuple-element.6.nt_ref), custom_call_target="tpu_custom_call" | custom-call | tf_op jit(solution)/shard_map/tokens_there/pallas_call | solution.py:410
  198.8 0.0 slice-done
  198.8 0.0 slice-done.1
  198.8 2.4 slice.36
  201.2 10.8 %reshape.44 = bf16[1152,3,576]{2,1,0:T(4,128)(2,1)} reshape(bf16[32,36,1728]{2,1,0:T(8,128)(2,1)} %slice.36) | data formatting | bytes 7962624 | tf_op jit(solution)/shard_map/reshape | solution.py:157
  212.0 11.3 %copy.16 = bf16[1152,3,576]{0,2,1:T(8,128)(2,1)} copy(bf16[1152,3,576]{2,1,0:T(4,128)(2,1)} %reshape.44) | data formatting | bytes 7962624
  223.3 4.6 %pad.25.clone = bf16[1152,3,640]{0,2,1:T(8,128)(2,1)} pad(bf16[1152,3,576]{0,2,1:T(8,128)(2,1)} %copy.16, bf16[]{:T(256)} %constant.2.clone.1), padding=0_0x0_0x0_64 | pad | bytes 8404994 | tf_op jit(solution)/shard_map/jit(_pad)/pad | solution.py:158
  228.0 6.6 %copy.14.wq_ref = bf16[1152,1920]{1,0:T(8,128)(2,1)} copy(bf16[1152,1920]{0,1:T(8,128)(2,1)} %bitcast.17) | data formatting | bytes 8847360 | tf_op jit(solution)/shard_map/reshape | solution.py:158
  235.3 24.9 %temporal.1.a_ref = bf16[6,8,16,640]{3,2,1,0:T(8,128)(2,1)} custom-call(s32[1]{0:T(128)S(6)} %copy.17.total_ref, bf16[6,8,16,1152]{3,2,1,0:T(8,128)(2,1)} %tokens_there.1.x_ref, bf16[1152,1920]{1,0:T(8,128)(2,1)} %copy.14.wq_ref), custom_call_target="tpu_custom_call" | custom-call | tf_op jit(solution)/shard_map/temporal/pallas_call | solution.py:288
  260.2 16.8 %tokens_back.1.att_ref = bf16[8,128,640]{2,1,0:T(8,128)(2,1)} custom-call(bf16[6,8,16,640]{3,2,1,0:T(8,128)(2,1)} %temporal.1.a_ref), custom_call_target="tpu_custom_call" | custom-call | tf_op jit(solution)/shard_map/tokens_back/pallas_call | solution.py:410
  277.0 2.0 slice.37
  279.0 2.2 reshape.46
  281.2 1.2 pad.26.wo_ref
  282.4 5.4 %finish.1 = (bf16[8,128,1152]{2,1,0:T(8,128)(2,1)}, bf16[8,80,1152]{2,1,0:T(8,128)(2,1)}) custom-call(s32[1]{0:T(128)S(6)} %copy.17.total_ref, bf16[8,128,640]{2,1,0:T(8,128)(2,1)} %tokens_back.1.att_ref, bf16[8,128,1152]{2,1,0:T(8,128)(2,1)} %get-tuple-element.7.mid_ref, bf16[8,128,1152]{2,1,0:T(8,128)(2,1)} %bitcast.18, f32[2,1152]{1,0:T(2,128)} %bitcast.22, ...), custom_call_target="tpu_custom_call" | custom-call | tf_op jit(solution)/shard_map/finish/pallas_call | solution.py:335
  287.8 39.8 %reduce_gradient.1 = f32[48,128]{1,0:T(8,128)} custom-call(bf16[4,2,80,1152]{3,2,1,0:T(8,128)(2,1)} %bitcast.20), custom_call_target="tpu_custom_call" | custom-call | tf_op jit(solution)/shard_map/reduce_gradient/pallas_call | solution.py:510
  327.6 1.3 slice.33
  (2 shorter events, 0.0 us)
Async XLA Ops:
  133.3 65.4 %slice-start = ((s8[5505024]{0:T(1024)(128)(4,1)}), s8[4194304]{0:T(1024)(128)(4,1)S(1)}, s32[]{:S(2)}) async-start(s8[5505024]{0:T(1024)(128)(4,1)} %bitcast.11), calls=%async_computation | async-start | bytes 8388608
  134.7 64.1 %slice-start.1 = ((s8[5505024]{0:T(1024)(128)(4,1)}), s8[1310720]{0:T(1024)(128)(4,1)S(1)}, s32[]{:S(2)}) async-start(s8[5505024]{0:T(1024)(128)(4,1)} %bitcast.11), calls=%async_computation.1 | async-start | bytes 2621440

commit v2 on v0

v2 whole, which is shorter than its diff:
```python
import math

import jax
import jax.numpy as jnp
from jax import lax
from jax.experimental import pallas as pl
from jax.experimental.pallas import tpu as pltpu
from jax.sharding import PartitionSpec as P

MESH = pl.DeviceIdType.MESH
BF = jnp.bfloat16
F32 = jnp.float32
HDIM = 72
WIDTH = 1152
INNER = 576
PAD = 640
PIX = 128
SLOTS = 8
OWN = 16
SENDERS = 6
PACK = 1792
SCALE = math.log2(math.e) / math.sqrt(HDIM)
BATCH = 2
GROUPS = 8
ANY = pl.BlockSpec(memory_space=pl.ANY)
VM = pl.BlockSpec(memory_space=pltpu.VMEM)
SM = pl.BlockSpec(memory_space=pltpu.SMEM)
BIG = 56 * 1024 * 1024


def greet(partners):
    barrier = pltpu.get_barrier_semaphore()
    for who in partners:
        pl.semaphore_signal(barrier, inc=1, device_id=who, device_id_type=MESH)
    pl.semaphore_wait(barrier, len(partners))


def pack(qkv_ref, out_ref):
    qkv, out = qkv_ref[...].astype(F32), out_ref[...].astype(F32)
    k, v = qkv[:, INNER : 2 * INNER], qkv[:, 2 * INNER :]
    top = jnp.concatenate([qkv[:, :INNER], k[:, 512:], k[:, :512], v, jnp.zeros((36, 64), F32)], axis=1)
    blank = jnp.zeros((6, 64), F32)
    side = jnp.concatenate([
        jnp.concatenate([out[12:, :INNER], blank], axis=1),
        jnp.concatenate([blank, out[12:, INNER:]], axis=1),
    ], axis=0)
    low = jnp.concatenate([out[:12], side], axis=1)
    return jnp.concatenate([top, low], axis=0).astype(BF)


BOTH_WAYS = (
    ((), ("az1", "by1u", "by1d", "by2", "bz10", "ay1u0", "ay1d0")),
    (("az1",), ("az2", "ay1u1", "ay1d1")),
    (("by1u", "by1d"), ("bz11", "bz12")),
    (("bz10",), ("bz20",)),
    (("by2",), ("bz13",)),
    (("ay1u0", "ay1d0"), ("ay2u0", "ay2d0")),
    (("az2",), ("az3", "ay1u2", "ay1d2")),
    (("bz20",), ("bz30",)),
    (("bz11",), ("bz21",)),
    (("ay1u1", "ay1d1"), ("ay2u1", "ay2d1")),
    (("az3",), ("ay1u3", "ay1d3")),
    (("bz12",), ("bz22",)),
    (("bz30",), ("bz40",)),
    (("bz21",), ("bz31",)),
    (("ay2u0", "ay2d0"), ("as0",)),
    (("bz13",), ("bz23",)),
    (("ay1u2", "ay1d2"), ("ay2u2", "ay2d2")),
    (("bz22",), ("bz32",)),
    (("bz40",), ("bs0",)),
    (("bz31",), ("bz41",)),
    (("ay2u1", "ay2d1"), ("as1",)),
    (("ay1u3", "ay1d3"), ("ay2u3", "ay2d3")),
    (("bz23",), ("bz33",)),
    (("bz32",), ("bz42",)),
    (("bz41",), ("bs1",)),
    (("ay2u2", "ay2d2"), ("as2",)),
    (("bz33",), ("bz43",)),
    (("bz42",), ("bs2",)),
    (("ay2u3", "ay2d3"), ("as3",)),
    (("bz43",), ("bs3",)),
)
ONE_WAY = (
    ((), ("az1", "ay1u0", "ay1d0")),
    (("az1",), ("az2", "ay1u1", "ay1d1")),
    (("az2",), ("az3", "ay1u2", "ay1d2")),
    (("ay1u0", "ay1d0"), ("ay2u0", "ay2d0")),
    (("az3",), ("ay1u3", "ay1d3")),
    (("ay1u1", "ay1d1"), ("ay2u1", "ay2d1")),
    (("ay2u0", "ay2d0"), ("as0",)),
    (("ay1u2", "ay1d2"), ("ay2u2", "ay2d2")),
    (("ay2u1", "ay2d1"), ("as1",)),
    (("ay1u3", "ay1d3"), ("ay2u3", "ay2d3")),
    (("ay2u2", "ay2d2"), ("as2",)),
    (("ay2u3", "ay2d3"), ("as3",)),
)


def gather_plan(full, ssem, rsem, split, order):
    grp, sp = lax.axis_index("grp"), lax.axis_index("sp")
    h, y, c = grp // 8, (grp // 2) % 4, grp % 2
    low = sp % 2
    up, down, far = lax.rem(y + 1, 4), lax.rem(y + 3, 4), lax.rem(y + 2, 4)
    hx = lax.rem(h + 3 + 2 * low, 4)
    hp = lax.rem(h + 5 - 2 * low, 4)
    hf = lax.rem(h + 2, 4)
    sibling = (grp + 1 - 2 * c, sp)
    y_up = ((h * 4 + up) * 2 + c, sp)
    y_down = ((h * 4 + down) * 2 + c, sp)
    y_far = ((h * 4 + far) * 2 + c, sp)
    pair = (grp, sp + 1 - 2 * low)
    cross = (hx * 8 + y * 2 + c, sp + 1 - 2 * low)
    al = slice(None)
    ca, a1, a2 = pl.ds(0, split), pl.ds(0, split // 2), pl.ds(split // 2, split // 2)
    table = {}

    def add(name, where, who):
        table[name] = (len(table), where, who)

    hs, ys = (h, hx, hp, hf), (y, up, down, far)
    add("az1", (h, y, c, al, ca), cross)
    add("az2", (hx, y, c, al, ca), pair)
    add("az3", (hp, y, c, al, ca), cross)
    for k in range(4):
        add(f"ay1u{k}", (hs[k], y, c, al, ca), y_up)
        add(f"ay1d{k}", (hs[k], y, c, al, ca), y_down)
        add(f"ay2u{k}", (hs[k], down, c, al, a1), y_up)
        add(f"ay2d{k}", (hs[k], up, c, al, a2), y_down)
        add(f"as{k}", (hs[k], al, c, al, ca), sibling)
    if split < PACK:
        rest = PACK - split
        cb = pl.ds(split, rest)

        def part(which):
            return pl.ds(pl.multiple_of(split + which * (rest // 2), 128), rest // 2)

        add("by1u", (h, y, c, al, cb), y_up)
        add("by1d", (h, y, c, al, cb), y_down)
        add("by2", (h, y, c, al, cb), y_far)
        for k in range(4):
            add(f"bz1{k}", (h, ys[k], c, al, cb), cross)
            add(f"bz2{k}", (hx, ys[k], c, al, cb), pair)
            add(f"bz3{k}", (hp, ys[k], c, al, part(1 - low)), cross)
            add(f"bz4{k}", (hf, ys[k], c, al, part(low)), pair)
            add(f"bs{k}", (al, ys[k], c, al, cb), sibling)

    def copy(name):
        i, where, who = table[name]
        return pltpu.make_async_remote_copy(
            src_ref=full.at[where], dst_ref=full.at[where], send_sem=ssem.at[i], recv_sem=rsem.at[i],
            device_id=who, device_id_type=MESH)

    def step(waits, starts):
        def run():
            for name in waits:
                copy(name).wait_recv()
            for name in starts:
                copy(name).start()
        return run

    def settle():
        for name in table:
            if name[1] == "s":
                copy(name).wait_recv()

    def drain():
        for name in table:
            copy(name).wait_send()

    partners = [sibling, y_up, y_down, y_far, pair, cross]
    return [step(*pair_of) for pair_of in order], settle, drain, (h, y, c), partners


COPIES = 46
SPLIT = 768


def iota(shape, dim):
    return lax.broadcasted_iota(jnp.int32, shape, dim)


def picks(condition):
    return condition.astype(F32).astype(BF)


def unpack(full, wq, wo):
    col, row = iota((144, 192), 1), iota((144, 192), 0)
    of, at = col // 48, col % 48
    top = picks((at < 36) & (36 * of + at == row))
    col, row = iota((72, 192), 1), iota((72, 192), 0)
    of, at = col // 48, col % 48 - 36
    main = picks((at >= 0) & (18 * of + at == row))
    left = picks((at >= 0) & (at < 6) & (18 * of + 12 + at == row))
    right = picks((at >= 6) & (18 * of + 6 + at == row))
    keep = iota((144, 128), 1) < 64

    @pl.loop(0, 4)
    def _(h):
        outs = []
        for i in range(2):
            block = full[h, 2 * i : 2 * i + 2].reshape(192, PACK)
            got = jnp.dot(top, block, preferred_element_type=F32)
            rows = pl.ds(pl.multiple_of((2 * h + i) * 144, 16), 144)
            mixed = got[:, 512:640]
            turned = jnp.concatenate([mixed[:, 64:], mixed[:, :64]], axis=1)
            wq[rows, 0:512] = got[:, 0:512].astype(BF)
            wq[rows, 512:640] = jnp.where(keep, mixed, 0.0).astype(BF)
            wq[rows, 640:1152] = got[:, 640:1152].astype(BF)
            wq[rows, 1152:1280] = jnp.where(keep, turned, 0.0).astype(BF)
            wq[rows, 1280:1920] = got[:, 1152:1792].astype(BF)
            whole = jnp.dot(main, block[:, :WIDTH], preferred_element_type=F32)
            side = block[:, WIDTH:]
            one = jnp.dot(left, side, preferred_element_type=F32)
            two = jnp.dot(right, side, preferred_element_type=F32)
            blank = jnp.zeros((72, 512), F32)
            outs.append(whole + jnp.concatenate([one, blank], axis=1) + jnp.concatenate([blank, two], axis=1))
        wo[pl.ds(pl.multiple_of(144 * h, 16), 144), :] = jnp.concatenate(outs, axis=0).astype(BF)

    wo[INNER:, :] = jnp.zeros((PAD - INNER, WIDTH), BF)


def modulated(x, offsets, shift_row, scale_row):
    mean = jnp.sum(x, axis=-1, keepdims=True) * (1.0 / WIDTH)
    x = x - mean
    spread = jnp.sum(x * x, axis=-1, keepdims=True) * (1.0 / WIDTH)
    x = x * lax.rsqrt(spread + 1e-06)
    return (x * (1.0 + offsets[scale_row]) + offsets[shift_row]).astype(BF)


def head_masks(j):
    lane = iota((1, 256), 1)
    start = 16 * j
    one = picks((lane >= start) & (lane < start + HDIM))
    two = picks((lane >= start + HDIM) & (lane < start + 2 * HDIM))
    return one, two


def attention(load, keys, valid):
    blocks = [None] * 5
    fill = [] if keys == PIX else [jnp.zeros((PIX - keys, 256), BF)]
    for j in range(4):
        one, two = head_masks(j)
        q, k, v = (load(part * PAD + 128 * j) for part in range(3))
        kk = jnp.concatenate([k * one, *fill, k * two, *fill], axis=0)
        vv = jnp.concatenate([v * one, *fill, v * two, *fill], axis=0)
        heads = jnp.concatenate(
            [jnp.broadcast_to(one, (PIX, 256)), jnp.broadcast_to(two, (PIX, 256))], axis=0)
        s = lax.dot_general(q, kk, (((1,), (1,)), ((), ())), preferred_element_type=F32)
        expo = []
        for part in (s[:, :128], s[:, 128:]):
            if valid is not None:
                part = jnp.where(valid, part, -1e30)
            top = jnp.max(part, axis=-1, keepdims=True)
            expo.append(jnp.exp2((part - top) * SCALE).astype(BF))
        expo = jnp.concatenate(expo, axis=1)
        o = jnp.dot(expo, vv, preferred_element_type=F32)
        total = jnp.dot(expo, heads, preferred_element_type=F32)
        o = o * (1.0 / jnp.where(total == 0.0, 1.0, total))
        for i, piece in ((j, o[:, :128]), (j + 1, o[:, 128:])):
            blocks[i] = piece if blocks[i] is None else blocks[i] + piece
    return jnp.concatenate(blocks, axis=1).astype(BF)


def shuffle(back):
    there, here = iota((128, 128), 1 if back else 0), iota((128, 128), 0 if back else 1)
    return picks(here == (there % 8) * OWN + there // 8)


def block_kernel(
    total_ref, shift_ref, gate_ref, hidden_ref, cot_in_ref, w1_ref, w2_ref, w3_ref, w4_ref,
    out_ref, grad_ref,
    full_s, full_t, wq, wo, hid, nrm, mid, nt, cot, qkv, att2, x_in, qkv_n, qkv_t, ap, attp, att,
    g_part, r0, red, r1, flipped, buf, r2,
    gs_s, gr_s, gs_t, gr_t, load_sem, there_s, there_r, there_l, back_s, back_r,
    s0, t0, s1, t1, s2, t2, out_sem,
):
    grp, sp = lax.axis_index("grp"), lax.axis_index("sp")
    c, low, chip = grp % 2, sp % 2, grp // 2
    sibling = (grp + 1 - 2 * c, sp)
    slot = lax.rem(sp, SENDERS)
    busy = sp < SENDERS
    offsets = [shift_ref[i : i + 1, :] for i in range(4)]
    total = total_ref[0]

    steps_s, settle_s, drain_s, here, partners = gather_plan(full_s, gs_s, gr_s, SPLIT, BOTH_WAYS)
    steps_t, settle_t, drain_t, _, _ = gather_plan(full_t, gs_t, gr_t, PACK, ONE_WAY)
    loads = [
        pltpu.make_async_copy(hidden_ref, hid, load_sem.at[0]),
        pltpu.make_async_copy(cot_in_ref, cot, load_sem.at[1]),
    ]
    for load in loads:
        load.start()
    full_s[here] = pack(w1_ref, w2_ref)
    full_t[here] = pack(w3_ref, w4_ref)
    greet_all = [(lax.rem(grp + d, 32), sp) for d in range(1, 32)]
    greet_all += [(grp, lax.rem(sp + d, 8)) for d in range(1, 8)] + [partners[-1]]
    greet(greet_all)
    steps_s[0]()
    loads[0].wait()

    @pl.loop(0, SLOTS)
    def _(f):
        @pl.when(busy)
        def _():
            nrm[f] = modulated(hid[f].astype(F32), offsets, 0, 1)

        for i in range(SLOTS):
            @pl.when(f == i)
            def _(i=i):
                for run in steps_s[1 + i : 2 + i]:
                    run()

    for run in steps_s[9:22]:
        run()
    steps_t[0]()
    for run in steps_s[22:]:
        run()
    steps_t[1]()
    settle_s()

    @pl.when(busy)
    def _():
        unpack(full_s, wq, wo)

    def there(i, d):
        to = lax.rem(sp + d, 8)
        frames = pl.ds(BATCH * i, BATCH)
        return pltpu.make_async_remote_copy(
            src_ref=nt.at[frames, pl.ds(pl.multiple_of(to * OWN, OWN), OWN), :],
            dst_ref=x_in.at[slot, frames], send_sem=there_s.at[i, d], recv_sem=there_r.at[i, d],
            device_id=(grp, to), device_id_type=MESH)

    def there_own(i):
        frames = pl.ds(BATCH * i, BATCH)
        return pltpu.make_async_copy(
            nt.at[frames, pl.ds(pl.multiple_of(sp * OWN, OWN), OWN), :], x_in.at[slot, frames], there_l.at[i])

    rest = steps_t[2:]

    @pl.loop(0, SLOTS // BATCH)
    def _(i):
        def beside(part):
            for n in range(SLOTS // BATCH):
                chosen = rest[3 * n + part : 3 * n + part + 1]
                if chosen:
                    @pl.when(i == n)
                    def _(chosen=chosen):
                        for run in chosen:
                            run()

        @pl.when(busy)
        def _():
            rows = nrm[pl.ds(BATCH * i, BATCH)].reshape(BATCH * PIX, WIDTH)
            got = jnp.dot(rows, wq[...], preferred_element_type=F32)
            qkv[...] = got.astype(BF).reshape(BATCH, PIX, 3 * PAD)

        beside(0)

        @pl.when(busy)
        def _():
            for u in range(BATCH):
                att2[u] = attention(lambda first: qkv[u, :, first : first + 256], PIX, None)

        beside(1)

        @pl.when(busy)
        def _():
            for u in range(BATCH):
                f = BATCH * i + u
                branch = jnp.dot(att2[u], wo[...], preferred_element_type=F32)
                middle = (hid[f].astype(F32) + gate_ref[0:1, :] * branch).astype(BF)
                mid[f] = middle
                nt[f] = modulated(middle.astype(F32), offsets, 2, 3)
            for d in (4, 3, 5, 2, 6, 1, 7):
                there(i, d).start()
            there_own(i).start()

        beside(2)

    settle_t()
    unpack(full_t, wq, wo)

    rows = SENDERS * 16

    @pl.loop(0, SLOTS // BATCH)
    def _(i):
        @pl.when((i == SLOTS // BATCH - 1) & busy)
        def _():
            loads[1].wait()

            @pl.loop(0, SLOTS)
            def _(f):
                kept = sp * SLOTS + f < total
                nrm[f] = jnp.where(kept, gate_ref[1:2, :] * cot[f].astype(F32), 0.0).astype(BF)

        for d in range(1, 8):
            @pl.when(lax.rem(sp + 8 - d, 8) < SENDERS)
            def _(d=d):
                there(i, d).wait_recv()

        @pl.when(busy)
        def _():
            there_own(i).wait()

        got = jnp.dot(
            x_in[:, pl.ds(BATCH * i, BATCH)].reshape(SENDERS * BATCH * OWN, WIDTH), wq[...],
            preferred_element_type=F32)
        lines = pl.ds(pl.multiple_of(i * BATCH * OWN, 16), BATCH * OWN)
        qkv_n[:, lines, :] = got.astype(BF).reshape(SENDERS, BATCH * OWN, 3 * PAD)

    @pl.when(sp >= SENDERS)
    def _():
        loads[1].wait()

    order = shuffle(False)

    @pl.loop(0, SENDERS)
    def _(s):
        got = jnp.dot(order, qkv_n[s], preferred_element_type=F32).astype(BF)
        qkv_t[:, s] = got.reshape(GROUPS, 16, 3 * PAD)

    key, row = iota((rows, PIX), 1), iota((rows, PIX), 0)
    frame = (key // 16) * 8 + key % 8
    valid = (key < rows) & (frame < total) & ((key // 8) % 2 == (row // 8) % 2)

    def back(i, d):
        to = lax.rem(sp + d, 8)
        pairs = pl.ds(2 * i, 2)
        return pltpu.make_async_remote_copy(
            src_ref=ap.at[lax.rem(to, SENDERS), pairs], dst_ref=attp.at[sp, pairs],
            send_sem=back_s.at[i, d], recv_sem=back_r.at[i, d],
            device_id=(grp, to), device_id_type=MESH)

    @pl.loop(0, GROUPS // 2)
    def _(i):
        for u in range(2):
            mixed = attention(
                lambda first: qkv_t[2 * i + u, :, :, first : first + 256].reshape(rows, 256), rows, valid)
            ap[:, 2 * i + u] = mixed.reshape(SENDERS, 16, PAD)
        for d in (4, 3, 5, 2, 6, 1, 7):
            @pl.when(lax.rem(sp + d, 8) < SENDERS)
            def _(d=d):
                back(i, d).start()

        @pl.when(busy)
        def _():
            attp[sp, pl.ds(2 * i, 2)] = ap[slot, pl.ds(2 * i, 2)]

    swap = pltpu.make_async_remote_copy(
        src_ref=g_part.at[:, 1 - c], dst_ref=r0, send_sem=s0, recv_sem=t0, device_id=sibling, device_id_type=MESH)

    def step1(to_x):
        return pltpu.make_async_remote_copy(
            src_ref=red.at[to_x], dst_ref=r1.at[slot], send_sem=s1.at[to_x], recv_sem=t1.at[slot],
            device_id=(grp, 2 * to_x + c), device_id_type=MESH)

    def step2(d):
        to = lax.rem(grp + d, 32)
        return pltpu.make_async_remote_copy(
            src_ref=buf.at[to], dst_ref=r2.at[chip], send_sem=s2.at[d], recv_sem=t2.at[d],
            device_id=(to, sp), device_id_type=MESH)

    def output(f):
        kept = sp * SLOTS + f < total
        branch = jnp.dot(att[f], wo[...], preferred_element_type=F32)
        out = mid[f].astype(F32) + gate_ref[1:2, :] * branch
        hid[f] = jnp.where(kept, out, 0.0).astype(BF)

    @pl.when(busy)
    def _():
        for i in range(GROUPS // 2):
            for d in range(1, 8):
                back(i, d).wait_recv()
        unorder = shuffle(True)

        @pl.loop(0, 8)
        def _(t):
            got = jnp.dot(unorder, attp[t].reshape(128, PAD), preferred_element_type=F32).astype(BF)
            att[:, pl.ds(pl.multiple_of(t * OWN, OWN), OWN), :] = got.reshape(SLOTS, OWN, PAD)

        @pl.loop(0, 3)
        def _(n):
            cols = pl.ds(pl.multiple_of(n * 384, 128), 384)
            got = lax.dot_general(
                att[...].reshape(SLOTS * PIX, PAD), nrm[:, :, cols].reshape(SLOTS * PIX, 384),
                (((0,), (0,)), ((), ())), preferred_element_type=F32) * (1.0 / PIX)
            for t in range(8):
                part = jnp.concatenate([got[72 * t : 72 * t + 72], jnp.zeros((8, 384), F32)], axis=0)
                g_part[t // 2, t % 2, :, cols] = part.astype(BF)

        swap.start()

        @pl.loop(0, SLOTS // 2)
        def _(f):
            output(f)

        swap.wait()
        for i in range(4):
            red[i] = (g_part[i, c].astype(F32) + r0[i].astype(F32)).astype(BF)
        for i in range(4):
            @pl.when(2 * i + c != sp)
            def _(i=i):
                step1(i).start()

            @pl.when(2 * i + c == sp)
            def _(i=i):
                r1[slot] = red[i]

        @pl.loop(SLOTS // 2, SLOTS)
        def _(f):
            output(f)

    @pl.when(sp >= SENDERS)
    def _():
        hid[...] = jnp.zeros_like(hid)

    result = pltpu.make_async_copy(hid, out_ref, out_sem)
    result.start()

    @pl.when(low == c)
    def _():
        for s in range(SENDERS):
            @pl.when(sp != s)
            def _(s=s):
                pltpu.make_async_remote_copy(
                    src_ref=red.at[0], dst_ref=r1.at[s], send_sem=s1.at[0], recv_sem=t1.at[s],
                    device_id=sibling, device_id_type=MESH).wait_recv()

        whole = r1[0].astype(F32)
        for s in range(1, SENDERS):
            whole = whole + r1[s].astype(F32)
        whole = jnp.concatenate([whole, jnp.zeros((48, WIDTH), F32)], axis=0)
        for n in range(9):
            flipped[128 * n : 128 * n + 128] = whole[:, 128 * n : 128 * n + 128].T
        for g in range(32):
            part = jnp.concatenate([flipped[36 * g : 36 * g + 36], jnp.zeros((12, 128), F32)], axis=0)
            buf[g] = part.astype(BF)

        @pl.loop(1, 32)
        def _(d):
            step2(d).start()

        r2[chip] = buf[grp]

        @pl.loop(1, 32)
        def _(d):
            step2(d).wait_send()

    @pl.loop(1, 32)
    def _(d):
        @pl.when(lax.rem(grp + 32 - d, 2) == low)
        def _():
            step2(d).wait_recv()

    whole = r2[0].astype(F32)
    for i in range(1, 16):
        whole = whole + r2[i].astype(F32)
    grad_ref[...] = whole[:36, :HDIM]

    drain_s()
    drain_t()

    @pl.when(busy)
    def _():
        for i in range(4):
            @pl.when(2 * i + c != sp)
            def _(i=i):
                step1(i).wait_send()

        for i in range(SLOTS // BATCH):
            for d in range(1, 8):
                there(i, d).wait_send()

    for i in range(GROUPS // 2):
        for d in range(1, 8):
            @pl.when(lax.rem(sp + d, 8) < SENDERS)
            def _(d=d, i=i):
                back(i, d).wait_send()

    result.wait()


def on_device(
    hidden,
    frame_counts,
    shifts,
    gates,
    w_qkv_spatial,
    w_out_spatial,
    w_qkv_temporal,
    w_out_temporal,
    cotangent,
):
    frames = (SLOTS, PIX, WIDTH)
    dma = pltpu.SemaphoreType.DMA
    block_out, grad = pl.pallas_call(
        block_kernel,
        out_shape=(jax.ShapeDtypeStruct(frames, BF), jax.ShapeDtypeStruct((36, HDIM), F32)),
        in_specs=[SM, VM, VM, ANY, ANY, VM, VM, VM, VM],
        out_specs=(ANY, VM),
        scratch_shapes=[
            pltpu.VMEM((4, 4, 2, 48, PACK), BF),
            pltpu.VMEM((4, 4, 2, 48, PACK), BF),
            pltpu.VMEM((WIDTH, 3 * PAD), BF),
            pltpu.VMEM((PAD, WIDTH), BF),
            *[pltpu.VMEM(frames, BF)] * 5,
            pltpu.VMEM((BATCH, PIX, 3 * PAD), BF),
            pltpu.VMEM((BATCH, PIX, PAD), BF),
            pltpu.VMEM((SENDERS, SLOTS, OWN, WIDTH), BF),
            pltpu.VMEM((SENDERS, 128, 3 * PAD), BF),
            pltpu.VMEM((GROUPS, SENDERS, 16, 3 * PAD), BF),
            pltpu.VMEM((SENDERS, GROUPS, 16, PAD), BF),
            pltpu.VMEM((8, GROUPS, 16, PAD), BF),
            pltpu.VMEM((SLOTS, PIX, PAD), BF),
            pltpu.VMEM((4, 2, 80, WIDTH), BF),
            pltpu.VMEM((4, 80, WIDTH), BF),
            pltpu.VMEM((4, 80, WIDTH), BF),
            pltpu.VMEM((SENDERS, 80, WIDTH), BF),
            pltpu.VMEM((WIDTH, 128), F32),
            pltpu.VMEM((32, 48, 128), BF),
            pltpu.VMEM((16, 48, 128), BF),
            dma((COPIES,)), dma((COPIES,)), dma((COPIES,)), dma((COPIES,)),
            dma((2,)),
            dma((4, 8)), dma((4, 8)), dma((4,)),
            dma((4, 8)), dma((4, 8)),
            dma, dma, dma((4,)), dma((SENDERS,)), dma((32,)), dma((32,)), dma,
        ],
        compiler_params=pltpu.CompilerParams(
            vmem_limit_bytes=BIG, collective_id=1, has_side_effects=True),
        name="block",
    )(
        frame_counts, shifts[0], gates[0], hidden[0], cotangent[0],
        w_qkv_spatial, w_out_spatial, w_qkv_temporal, w_out_temporal,
    )
    return block_out[None], grad


def solution(mesh):
    return jax.shard_map(
        on_device,
        mesh=mesh,
        in_specs=(
            P("grp", "sp", None, None),
            P("grp"),
            P("grp", None, None),
            P("grp", None, None),
            P("grp", None),
            P("grp", None),
            P("grp", None),
            P("grp", None),
            P("grp", "sp", None, None),
        ),
        out_specs=(P("grp", "sp", None, None), P("grp", "sp")),
        check_vma=False,
    )
```

time: 656 us -> 136 us (0.21)
  waiting for transfers between devices: 454 us -> 0 us
  Pallas kernels: 0 us -> 131 us
  starting transfers between devices: 83.4 us -> 0 us
  local copies, waits for them, and re-layouts: 65.7 us -> 3.88 us
  matrix products: 19.5 us -> 0 us
  between operations: 15.5 us -> 1.29 us
  other arithmetic: 8.43 us -> 0 us
    unnamed x8 -> x0, waiting for transfers between devices: 305 us -> none
    pallas_call x0 -> x1, Pallas kernels: none -> 131 us  [on_device(): pl.pallas_call(block_kernel, out_shape=(jax.ShapeDtypeStruct(frames, BF),...]
    all_gather x4 -> x0, waiting for transfers between devices: 116 us -> none  [the longest x1 58.8 us: on_device(): lax.all_gather(w_qkv_spatial, 'grp', axis=0, tiled=True)]
    all_to_all x2 -> x0, starting transfers between devices: 83.3 us -> none  [the longest x1 77.5 us: on_device(): lax.all_to_all(normed_t, 'sp', split_axis=1, concat_axis=0, tiled=True)]
    all_to_all x2 -> x0, waiting for transfers between devices: 33.7 us -> none  [the longest x1 22 us: on_device(): lax.all_to_all(normed_t, 'sp', split_axis=1, concat_axis=0, tiled=True)]
    unnamed x20 -> x4, local copies, waits for them, and re-layouts: 24.6 us -> 3.88 us
    dot_general x5 -> x0, matrix products: 19.5 us -> none  [the longest x1 6.33 us: on_device(): jnp.dot(pixel_rows.reshape(all_frames * own_pixels, width), proj_temporal...]
    convert_element_type x3 -> x0, local copies, waits for them, and re-layouts: 11.2 us -> none  [the longest x1 5.84 us: on_device(): projected_rows.astype(jnp.bfloat16)]
  transfers between devices with their start and end apart: 8 -> 0, of which waited for: 6 -> 0; matrix products, arithmetic and copies ran while one was open for 14% -> 0% of each run, Pallas kernels for 0% -> 0%
where the time goes in v2:
time: 136 us
  Pallas kernels  131 us (96%)
  local copies, waits for them, and re-layouts  3.88 us (3%)
    pallas_call x1, Pallas kernels, on_device(): pl.pallas_call(block_kernel, out_shape=(jax.ShapeDtypeStruct(frames, BF),...  131 us
    unnamed x4, local copies, waits for them, and re-layouts  3.88 us

profile of v2, /device:TPU:7, one launch (start us, length us, event | category | flops | bytes accessed | tf_op | source)
XLA Modules:
  0.0 135.7 jit_solution(7310910412065505615)
XLA Ops:
  1.3 130.6 %block.1 = (bf16[8,128,1152]{2,1,0:T(8,128)(2,1)}, f32[36,72]{1,0:T(8,128)}) custom-call(s32[1]{0:T(128)S(6)} %copy.13.total_ref, f32[4,1152]{1,0:T(4,128)} %bitcast.8, f32[2,1152]{1,0:T(2,128)} %bitcast.9, bf16[8,128,1152]{2,1,0:T(8,128)(2,1)} %bitcast.5, bf16[8,128,1152]{2,1,0:T(8,128)(2,1)} %bitcast.6, bf16[36,1728]{1,0:T(8,128)(2,1)} %w1_ref.1, ...), custom_call_target="tpu_custom_call" | custom-call | tf_op jit(solution)/shard_map/block/pallas_call | solution.py:596
  131.8 0.0 copy-start
  131.9 3.3 %copy.14 = bf16[1,8,128,1152]{3,2,1,0:T(8,128)(2,1)} copy(bf16[1,8,128,1152]{3,2,1,0:T(8,128)(2,1)} %bitcast.7) | data formatting | bytes 4718592
  135.1 0.0 copy-done
  135.1 0.6 copy.15
Async XLA Ops:
  131.8 3.3 %copy-start = (f32[36,72]{1,0:T(8,128)S(1)}, f32[36,72]{1,0:T(8,128)}, u32[]{:S(2)}) copy-start(f32[36,72]{1,0:T(8,128)} %get-tuple-element.9) | copy-start | bytes 31108

commit v3 on v2

v3 whole, which is shorter than its diff:
```python
import math

import jax
import jax.numpy as jnp
from jax import lax
from jax.experimental import pallas as pl
from jax.experimental.pallas import tpu as pltpu
from jax.sharding import PartitionSpec as P

MESH = pl.DeviceIdType.MESH
BF = jnp.bfloat16
F32 = jnp.float32
HDIM = 72
WIDTH = 1152
INNER = 576
PAD = 640
PIX = 128
SLOTS = 8
OWN = 16
SENDERS = 6
PACK = 1792
SCALE = math.log2(math.e) / math.sqrt(HDIM)
BATCH = 2
GROUPS = 8
ANY = pl.BlockSpec(memory_space=pl.ANY)
VM = pl.BlockSpec(memory_space=pltpu.VMEM)
SM = pl.BlockSpec(memory_space=pltpu.SMEM)
BIG = 56 * 1024 * 1024


def greet(partners):
    barrier = pltpu.get_barrier_semaphore()
    for who in partners:
        pl.semaphore_signal(barrier, inc=1, device_id=who, device_id_type=MESH)
    pl.semaphore_wait(barrier, len(partners))


def pack(qkv_ref, out_ref):
    qkv, out = qkv_ref[...].astype(F32), out_ref[...].astype(F32)
    k, v = qkv[:, INNER : 2 * INNER], qkv[:, 2 * INNER :]
    top = jnp.concatenate([qkv[:, :INNER], k[:, 512:], k[:, :512], v, jnp.zeros((36, 64), F32)], axis=1)
    blank = jnp.zeros((6, 64), F32)
    side = jnp.concatenate([
        jnp.concatenate([out[12:, :INNER], blank], axis=1),
        jnp.concatenate([blank, out[12:, INNER:]], axis=1),
    ], axis=0)
    low = jnp.concatenate([out[:12], side], axis=1)
    return jnp.concatenate([top, low], axis=0).astype(BF)


STEPS = (
    ((), ("z1p", "z1q", "upp0", "dnp0", "upq0", "dnq0")),
    (("z1p",), ("z2p", "upp1", "dnp1")),
    (("z1q",), ("z2q", "upq1", "dnq1")),
    (("upp0", "dnp0"), ("farp0",)),
    (("upq0", "dnq0"), ("farq0",)),
    (("z2p",), ("z3p", "upp2", "dnp2")),
    (("z2q",), ("z3q", "upq2", "dnq2")),
    (("upp1", "dnp1"), ("farp1",)),
    (("upq1", "dnq1"), ("farq1",)),
    (("z3p",), ("upp3", "dnp3")),
    (("z3q",), ("upq3", "dnq3")),
    (("farp0", "farq0"), ("s0",)),
    (("upp2", "dnp2"), ("farp2",)),
    (("upq2", "dnq2"), ("farq2",)),
    (("farp1", "farq1"), ("s1",)),
    (("upp3", "dnp3"), ("farp3",)),
    (("upq3", "dnq3"), ("farq3",)),
    (("farp2", "farq2"), ("s2",)),
    (("farp3", "farq3"), ("s3",)),
)


def gather_plan(full, ssem, rsem):
    grp, sp = lax.axis_index("grp"), lax.axis_index("sp")
    h, y, c = grp // 8, (grp // 2) % 4, grp % 2
    low = sp % 2
    up, down = lax.rem(y + 1, 4), lax.rem(y + 3, 4)
    hx = lax.rem(h + 3 + 2 * low, 4)
    hp = lax.rem(h + 5 - 2 * low, 4)
    hf = lax.rem(h + 2, 4)
    sibling = (grp + 1 - 2 * c, sp)
    y_up = ((h * 4 + up) * 2 + c, sp)
    y_down = ((h * 4 + down) * 2 + c, sp)
    pair = (grp, sp + 1 - 2 * low)
    cross = (hx * 8 + y * 2 + c, sp + 1 - 2 * low)
    al = slice(None)
    hs = (h, hx, hp, hf)
    table = {}

    def add(name, where, who):
        table[name] = (len(table), where, who)

    for stream, cols in (("p", pl.ds(0, PACK // 2)), ("q", pl.ds(PACK // 2, PACK // 2))):
        add("z1" + stream, (h, y, c, al, cols), cross)
        add("z2" + stream, (hx, y, c, al, cols), pair)
        add("z3" + stream, (hp, y, c, al, cols), cross)
        for k in range(4):
            add(f"up{stream}{k}", (hs[k], y, c, al, cols), y_up)
            add(f"dn{stream}{k}", (hs[k], y, c, al, cols), y_down)
            if stream == "p":
                add(f"farp{k}", (hs[k], down, c, al, cols), y_up)
            else:
                add(f"farq{k}", (hs[k], up, c, al, cols), y_down)
    for k in range(4):
        add(f"s{k}", (hs[k], al, c), sibling)

    def copy(name):
        i, where, who = table[name]
        return pltpu.make_async_remote_copy(
            src_ref=full.at[where], dst_ref=full.at[where], send_sem=ssem.at[i], recv_sem=rsem.at[i],
            device_id=who, device_id_type=MESH)

    def step(waits, starts):
        def run():
            for name in waits:
                copy(name).wait_recv()
            for name in starts:
                copy(name).start()
        return run

    def settle(k):
        copy(f"s{k}").wait_recv()
        return hs[k]

    def drain():
        for name in table:
            copy(name).wait_send()

    return [step(*both) for both in STEPS], settle, drain, (h, y, c), cross


COPIES = 34


def iota(shape, dim):
    return lax.broadcasted_iota(jnp.int32, shape, dim)


def picks(condition):
    return condition.astype(F32).astype(BF)


def unpack(full, settle, wq, wo):
    col, row = iota((144, 192), 1), iota((144, 192), 0)
    of, at = col // 48, col % 48
    top = picks((at < 36) & (36 * of + at == row))
    col, row = iota((72, 192), 1), iota((72, 192), 0)
    of, at = col // 48, col % 48 - 36
    main = picks((at >= 0) & (18 * of + at == row) & (at < 12))
    left = picks((at >= 0) & (at < 6) & (18 * of + 12 + at == row))
    right = picks((at >= 6) & (18 * of + 6 + at == row))
    keep = iota((144, 128), 1) < 64

    wo[INNER:, :] = jnp.zeros((PAD - INNER, WIDTH), BF)
    for k in range(4):
        h = settle(k)
        outs = []
        for i in range(2):
            block = full[h, 2 * i : 2 * i + 2].reshape(192, PACK)
            got = jnp.dot(top, block, preferred_element_type=F32)
            rows = pl.ds(pl.multiple_of((2 * h + i) * 144, 16), 144)
            mixed = got[:, 512:640]
            turned = jnp.concatenate([mixed[:, 64:], mixed[:, :64]], axis=1)
            wq[rows, 0:512] = got[:, 0:512].astype(BF)
            wq[rows, 512:640] = jnp.where(keep, mixed, 0.0).astype(BF)
            wq[rows, 640:1152] = got[:, 640:1152].astype(BF)
            wq[rows, 1152:1280] = jnp.where(keep, turned, 0.0).astype(BF)
            wq[rows, 1280:1920] = got[:, 1152:1792].astype(BF)
            whole = jnp.dot(main, block[:, :WIDTH], preferred_element_type=F32)
            side = block[:, WIDTH:]
            one = jnp.dot(left, side, preferred_element_type=F32)
            two = jnp.dot(right, side, preferred_element_type=F32)
            blank = jnp.zeros((72, 512), F32)
            outs.append(whole + jnp.concatenate([one, blank], axis=1) + jnp.concatenate([blank, two], axis=1))
        wo[pl.ds(pl.multiple_of(144 * h, 16), 144), :] = jnp.concatenate(outs, axis=0).astype(BF)


def modulated(x, offsets, shift_row, scale_row):
    mean = jnp.sum(x, axis=-1, keepdims=True) * (1.0 / WIDTH)
    x = x - mean
    spread = jnp.sum(x * x, axis=-1, keepdims=True) * (1.0 / WIDTH)
    x = x * lax.rsqrt(spread + 1e-06)
    return (x * (1.0 + offsets[scale_row]) + offsets[shift_row]).astype(BF)


def head_masks(j):
    lane = iota((1, 256), 1)
    start = 16 * j
    one = picks((lane >= start) & (lane < start + HDIM))
    two = picks((lane >= start + HDIM) & (lane < start + 2 * HDIM))
    return one, two


def attention(load, keys, valid):
    blocks = [None] * 5
    fill = [] if keys == PIX else [jnp.zeros((PIX - keys, 256), BF)]
    for j in range(4):
        one, two = head_masks(j)
        q, k, v = (load(part * PAD + 128 * j) for part in range(3))
        kk = jnp.concatenate([k * one, *fill, k * two, *fill], axis=0)
        vv = jnp.concatenate([v * one, *fill, v * two, *fill], axis=0)
        heads = jnp.concatenate(
            [jnp.broadcast_to(one, (PIX, 256)), jnp.broadcast_to(two, (PIX, 256))], axis=0)
        s = lax.dot_general(q, kk, (((1,), (1,)), ((), ())), preferred_element_type=F32)
        expo = []
        for part in (s[:, :128], s[:, 128:]):
            if valid is not None:
                part = jnp.where(valid, part, -1e30)
            top = jnp.max(part, axis=-1, keepdims=True)
            expo.append(jnp.exp2((part - top) * SCALE).astype(BF))
        expo = jnp.concatenate(expo, axis=1)
        o = jnp.dot(expo, vv, preferred_element_type=F32)
        total = jnp.dot(expo, heads, preferred_element_type=F32)
        o = o * (1.0 / jnp.where(total == 0.0, 1.0, total))
        for i, piece in ((j, o[:, :128]), (j + 1, o[:, 128:])):
            blocks[i] = piece if blocks[i] is None else blocks[i] + piece
    return jnp.concatenate(blocks, axis=1).astype(BF)


def shuffle(back):
    there, here = iota((128, 128), 1 if back else 0), iota((128, 128), 0 if back else 1)
    return picks(here == (there % 8) * OWN + there // 8)


def block_kernel(
    total_ref, shift_ref, gate_ref, hidden_ref, cot_in_ref, w1_ref, w2_ref, w3_ref, w4_ref,
    out_ref, grad_ref,
    full_s, full_t, wq, wo_s, wo_t, hid, nrm, mid, cot, qkv, att_s, x_in, a_in, xp, qkv_t, ap, attp, att,
    g_part, r0, red, r1, flipped, buf, r2,
    gs_s, gr_s, gs_t, gr_t, load_sem, early_s, early_r, there_s, there_r, there_l, back_s, back_r,
    s0, t0, s1, t1, s2, t2, out_sem,
):
    grp, sp = lax.axis_index("grp"), lax.axis_index("sp")
    c, low, chip = grp % 2, sp % 2, grp // 2
    sibling = (grp + 1 - 2 * c, sp)
    slot = lax.rem(sp, SENDERS)
    busy = sp < SENDERS
    offsets = [shift_ref[i : i + 1, :] for i in range(4)]
    total = total_ref[0]
    rows = SENDERS * 16
    batches = SLOTS // BATCH

    def from_me(d):
        return lax.rem(sp + d, 8)

    def pixels(rank):
        return pl.ds(pl.multiple_of(rank * OWN, OWN), OWN)

    def if_sends(d):
        return pl.when(lax.rem(sp + 8 - d, 8) < SENDERS)

    def if_gets(d):
        return pl.when(from_me(d) < SENDERS)

    def remote(src, dst, send_sem, recv_sem, who):
        return pltpu.make_async_remote_copy(
            src_ref=src, dst_ref=dst, send_sem=send_sem, recv_sem=recv_sem,
            device_id=who, device_id_type=MESH)

    def early(d):
        to = from_me(d)
        return remote(hidden_ref.at[:, pixels(to), :], x_in.at[slot], early_s.at[d], early_r.at[d], (grp, to))

    def there(i, d):
        to, frames = from_me(d), pl.ds(BATCH * i, BATCH)
        return remote(
            att_s.at[frames, pixels(to), :], a_in.at[slot, frames], there_s.at[i, d], there_r.at[i, d], (grp, to))

    def there_own(i):
        frames = pl.ds(BATCH * i, BATCH)
        return pltpu.make_async_copy(att_s.at[frames, pixels(sp), :], a_in.at[slot, frames], there_l.at[i])

    def back(i, d):
        to, pairs = from_me(d), pl.ds(2 * i, 2)
        return remote(
            ap.at[lax.rem(to, SENDERS), pairs], attp.at[sp, pairs], back_s.at[i, d], back_r.at[i, d], (grp, to))

    steps_s, settle_s, drain_s, here, cross = gather_plan(full_s, gs_s, gr_s)
    steps_t, settle_t, drain_t, _, _ = gather_plan(full_t, gs_t, gr_t)
    loads = [
        pltpu.make_async_copy(hidden_ref, hid, load_sem.at[0]),
        pltpu.make_async_copy(cot_in_ref, cot, load_sem.at[1]),
        pltpu.make_async_copy(hidden_ref.at[:, pixels(sp), :], x_in.at[slot], load_sem.at[2]),
    ]
    loads[0].start()
    loads[1].start()

    @pl.when(busy)
    def _():
        loads[2].start()

    full_s[here] = pack(w1_ref, w2_ref)
    full_t[here] = pack(w3_ref, w4_ref)
    greet_all = [(lax.rem(grp + d, 32), sp) for d in range(1, 32)]
    greet_all += [(grp, from_me(d)) for d in range(1, 8)] + [cross]
    greet(greet_all)
    steps_s[0]()

    @pl.when(busy)
    def _():
        for d in (4, 2, 6):
            early(d).start()

    loads[0].wait()
    loads[1].wait()

    @pl.loop(0, SLOTS)
    def _(f):
        @pl.when(busy)
        def _():
            nrm[f] = modulated(hid[f].astype(F32), offsets, 0, 1)

        for i in range(SLOTS):
            @pl.when(f == i)
            def _(i=i):
                steps_s[1 + i]()

        @pl.when((f == 1) & busy)
        def _():
            for d in (3, 5, 1, 7):
                early(d).start()

    for run in steps_s[9:17]:
        run()
    steps_t[0]()
    for run in steps_s[17:]:
        run()
    unpack(full_s, settle_s, wq, wo_s)

    rest = steps_t[1:]

    @pl.loop(0, batches)
    def _(i):
        @pl.when(busy)
        def _():
            tokens = nrm[pl.ds(BATCH * i, BATCH)].reshape(BATCH * PIX, WIDTH)
            got = jnp.dot(tokens, wq[...], preferred_element_type=F32)
            qkv[...] = got.astype(BF).reshape(BATCH, PIX, 3 * PAD)
            for u in range(BATCH):
                att_s[BATCH * i + u] = attention(lambda first: qkv[u, :, first : first + 256], PIX, None)
            for d in (4, 3, 5, 2, 6, 1, 7):
                there(i, d).start()
            there_own(i).start()

        for n in range(batches):
            @pl.when(i == n)
            def _(n=n):
                for run in rest[2 * n : 2 * n + 2]:
                    run()

    rest = rest[2 * batches :]

    for d in range(1, 8):
        @if_sends(d)
        def _(d=d):
            early(d).wait_recv()

    @pl.when(busy)
    def _():
        loads[2].wait()

    @pl.loop(0, batches)
    def _(i):
        for d in range(1, 8):
            @if_sends(d)
            def _(d=d):
                there(i, d).wait_recv()

        @pl.when(busy)
        def _():
            there_own(i).wait()

        frames = pl.ds(BATCH * i, BATCH)
        lines = SENDERS * BATCH * OWN
        branch = jnp.dot(a_in[:, frames].reshape(lines, PAD), wo_s[...], preferred_element_type=F32)
        middle = x_in[:, frames].reshape(lines, WIDTH).astype(F32) + gate_ref[0:1, :] * branch
        normed = modulated(middle.astype(BF).astype(F32), offsets, 2, 3)
        x_in[:, frames] = normed.reshape(SENDERS, BATCH, OWN, WIDTH)

        for n in range(batches):
            @pl.when(i == n)
            def _(n=n):
                for run in rest[n : n + 1]:
                    run()

    order = shuffle(False)

    @pl.loop(0, SENDERS)
    def _(s):
        got = jnp.dot(order, x_in[s].reshape(128, WIDTH), preferred_element_type=F32).astype(BF)
        xp[:, s] = got.reshape(GROUPS, 16, WIDTH)

    for run in rest[batches:]:
        run()
    unpack(full_t, settle_t, wq, wo_t)

    key, row = iota((rows, PIX), 1), iota((rows, PIX), 0)
    frame = (key // 16) * 8 + key % 8
    valid = (key < rows) & (frame < total) & ((key // 8) % 2 == (row // 8) % 2)

    @pl.loop(0, GROUPS // 2)
    def _(i):
        got = jnp.dot(xp[pl.ds(2 * i, 2)].reshape(2 * rows, WIDTH), wq[...], preferred_element_type=F32)
        qkv_t[...] = got.astype(BF).reshape(2, rows, 3 * PAD)
        for u in range(2):
            mixed = attention(lambda first: qkv_t[u, :, first : first + 256], rows, valid)
            ap[:, 2 * i + u] = mixed.reshape(SENDERS, 16, PAD)
        for d in (4, 3, 5, 2, 6, 1, 7):
            @if_gets(d)
            def _(d=d):
                back(i, d).start()

        @pl.when(busy)
        def _():
            attp[sp, pl.ds(2 * i, 2)] = ap[slot, pl.ds(2 * i, 2)]

    def swap(n):
        cols = pl.ds(384 * n, 384)
        return remote(g_part.at[:, 1 - c, :, cols], r0.at[:, :, cols], s0.at[n], t0.at[n], sibling)

    def step1(n, to_x):
        cols = pl.ds(384 * n, 384)
        return remote(
            red.at[to_x, :, cols], r1.at[slot, :, cols], s1.at[n, to_x], t1.at[n, slot], (grp, 2 * to_x + c))

    def step2(d):
        to = lax.rem(grp + d, 32)
        return remote(buf.at[to], r2.at[chip], s2.at[d], t2.at[d], (to, sp))

    @pl.when(busy)
    def _():
        @pl.loop(0, SLOTS)
        def _(f):
            kept = sp * SLOTS + f < total
            branch = jnp.dot(att_s[f], wo_s[...], preferred_element_type=F32)
            mid[f] = (hid[f].astype(F32) + gate_ref[0:1, :] * branch).astype(BF)
            nrm[f] = jnp.where(kept, gate_ref[1:2, :] * cot[f].astype(F32), 0.0).astype(BF)

        unorder = shuffle(True)
        for i in range(GROUPS // 2):
            for d in range(1, 8):
                back(i, d).wait_recv()

        @pl.loop(0, 8)
        def _(t):
            got = jnp.dot(unorder, attp[t].reshape(128, PAD), preferred_element_type=F32).astype(BF)
            att[:, pixels(t), :] = got.reshape(SLOTS, OWN, PAD)

        def gradient(n):
            cols = slice(384 * n, 384 * n + 384)
            got = lax.dot_general(
                att[...].reshape(SLOTS * PIX, PAD), nrm[:, :, cols].reshape(SLOTS * PIX, 384),
                (((0,), (0,)), ((), ())), preferred_element_type=F32) * (1.0 / PIX)
            for t in range(8):
                part = jnp.concatenate([got[72 * t : 72 * t + 72], jnp.zeros((8, 384), F32)], axis=0)
                g_part[t // 2, t % 2, :, cols] = part.astype(BF)
            swap(n).start()

        def pass_on(n):
            cols = slice(384 * n, 384 * n + 384)
            swap(n).wait()
            for i in range(4):
                red[i, :, cols] = (g_part[i, c, :, cols].astype(F32) + r0[i, :, cols].astype(F32)).astype(BF)
            for i in range(4):
                @pl.when(2 * i + c != sp)
                def _(i=i):
                    step1(n, i).start()

                @pl.when(2 * i + c == sp)
                def _(i=i):
                    r1[slot, :, cols] = red[i, :, cols]

        gradient(0)
        gradient(1)
        pass_on(0)
        gradient(2)
        pass_on(1)
        pass_on(2)

        @pl.loop(0, SLOTS)
        def _(f):
            kept = sp * SLOTS + f < total
            branch = jnp.dot(att[f], wo_t[...], preferred_element_type=F32)
            out = mid[f].astype(F32) + gate_ref[1:2, :] * branch
            hid[f] = jnp.where(kept, out, 0.0).astype(BF)

    @pl.when(sp >= SENDERS)
    def _():
        hid[...] = jnp.zeros_like(hid)

    result = pltpu.make_async_copy(hid, out_ref, out_sem)
    result.start()

    @pl.when(low == c)
    def _():
        for n in range(3):
            for s in range(SENDERS):
                @pl.when(sp != s)
                def _(n=n, s=s):
                    cols = pl.ds(384 * n, 384)
                    remote(
                        red.at[0, :, cols], r1.at[s, :, cols], s1.at[n, 0], t1.at[n, s], sibling).wait_recv()

        whole = r1[0].astype(F32)
        for s in range(1, SENDERS):
            whole = whole + r1[s].astype(F32)
        whole = jnp.concatenate([whole, jnp.zeros((48, WIDTH), F32)], axis=0)
        for n in range(9):
            flipped[128 * n : 128 * n + 128] = whole[:, 128 * n : 128 * n + 128].T
        for g in range(32):
            part = jnp.concatenate([flipped[36 * g : 36 * g + 36], jnp.zeros((12, 128), F32)], axis=0)
            buf[g] = part.astype(BF)

        @pl.loop(1, 32)
        def _(d):
            step2(d).start()

        r2[chip] = buf[grp]

        @pl.loop(1, 32)
        def _(d):
            step2(d).wait_send()

    @pl.loop(1, 32)
    def _(d):
        @pl.when(lax.rem(grp + 32 - d, 2) == low)
        def _():
            step2(d).wait_recv()

    whole = r2[0].astype(F32)
    for i in range(1, 16):
        whole = whole + r2[i].astype(F32)
    grad_ref[...] = whole[:36, :HDIM]

    drain_s()
    drain_t()

    @pl.when(busy)
    def _():
        for n in range(3):
            for i in range(4):
                @pl.when(2 * i + c != sp)
                def _(n=n, i=i):
                    step1(n, i).wait_send()

        for d in range(1, 8):
            early(d).wait_send()
            for i in range(batches):
                there(i, d).wait_send()

    for i in range(GROUPS // 2):
        for d in range(1, 8):
            @if_gets(d)
            def _(d=d, i=i):
                back(i, d).wait_send()

    result.wait()


def on_device(
    hidden,
    frame_counts,
    shifts,
    gates,
    w_qkv_spatial,
    w_out_spatial,
    w_qkv_temporal,
    w_out_temporal,
    cotangent,
):
    frames = (SLOTS, PIX, WIDTH)
    dma = pltpu.SemaphoreType.DMA
    block_out, grad = pl.pallas_call(
        block_kernel,
        out_shape=(jax.ShapeDtypeStruct(frames, BF), jax.ShapeDtypeStruct((36, HDIM), F32)),
        in_specs=[SM, VM, VM, ANY, ANY, VM, VM, VM, VM],
        out_specs=(ANY, VM),
        scratch_shapes=[
            pltpu.VMEM((4, 4, 2, 48, PACK), BF),
            pltpu.VMEM((4, 4, 2, 48, PACK), BF),
            pltpu.VMEM((WIDTH, 3 * PAD), BF),
            pltpu.VMEM((PAD, WIDTH), BF),
            pltpu.VMEM((PAD, WIDTH), BF),
            *[pltpu.VMEM(frames, BF)] * 4,
            pltpu.VMEM((BATCH, PIX, 3 * PAD), BF),
            pltpu.VMEM((SLOTS, PIX, PAD), BF),
            pltpu.VMEM((SENDERS, SLOTS, OWN, WIDTH), BF),
            pltpu.VMEM((SENDERS, SLOTS, OWN, PAD), BF),
            pltpu.VMEM((GROUPS, SENDERS, 16, WIDTH), BF),
            pltpu.VMEM((2, SENDERS * 16, 3 * PAD), BF),
            pltpu.VMEM((SENDERS, GROUPS, 16, PAD), BF),
            pltpu.VMEM((8, GROUPS, 16, PAD), BF),
            pltpu.VMEM((SLOTS, PIX, PAD), BF),
            pltpu.VMEM((4, 2, 80, WIDTH), BF),
            pltpu.VMEM((4, 80, WIDTH), BF),
            pltpu.VMEM((4, 80, WIDTH), BF),
            pltpu.VMEM((SENDERS, 80, WIDTH), BF),
            pltpu.VMEM((WIDTH, 128), F32),
            pltpu.VMEM((32, 48, 128), BF),
            pltpu.VMEM((16, 48, 128), BF),
            dma((COPIES,)), dma((COPIES,)), dma((COPIES,)), dma((COPIES,)),
            dma((3,)), dma((8,)), dma((8,)),
            dma((4, 8)), dma((4, 8)), dma((4,)),
            dma((4, 8)), dma((4, 8)),
            dma((3,)), dma((3,)), dma((3, 4)), dma((3, SENDERS)), dma((32,)), dma((32,)), dma,
        ],
        compiler_params=pltpu.CompilerParams(
            vmem_limit_bytes=BIG, collective_id=1, has_side_effects=True),
        name="block",
    )(
        frame_counts, shifts[0], gates[0], hidden[0], cotangent[0],
        w_qkv_spatial, w_out_spatial, w_qkv_temporal, w_out_temporal,
    )
    return block_out[None], grad


def solution(mesh):
    return jax.shard_map(
        on_device,
        mesh=mesh,
        in_specs=(
            P("grp", "sp", None, None),
            P("grp"),
            P("grp", None, None),
            P("grp", None, None),
            P("grp", None),
            P("grp", None),
            P("grp", None),
            P("grp", None),
            P("grp", "sp", None, None),
        ),
        out_specs=(P("grp", "sp", None, None), P("grp", "sp")),
        check_vma=False,
    )
```

time: 136 us -> 126 us (0.926)
  Pallas kernels: 131 us -> 120 us
    pallas_call x1, Pallas kernels: 131 us -> 120 us  [on_device(): pl.pallas_call(block_kernel, out_shape=(jax.ShapeDtypeStruct(frames, BF),...]
where the time goes in v3:
time: 126 us
  Pallas kernels  120 us (95%)
  local copies, waits for them, and re-layouts  3.88 us (3%)
  between operations  1.3 us (1%)
    pallas_call x1, Pallas kernels, on_device(): pl.pallas_call(block_kernel, out_shape=(jax.ShapeDtypeStruct(frames, BF),...  120 us
    unnamed x4, local copies, waits for them, and re-layouts  3.88 us

profile of v3, /device:TPU:7, one launch (start us, length us, event | category | flops | bytes accessed | tf_op | source)
XLA Modules:
  0.0 125.5 jit_solution(4636479850453464188)
XLA Ops:
  1.3 120.4 %block.1 = (bf16[8,128,1152]{2,1,0:T(8,128)(2,1)}, f32[36,72]{1,0:T(8,128)}) custom-call(s32[1]{0:T(128)S(6)} %copy.13.total_ref, f32[4,1152]{1,0:T(4,128)} %bitcast.8, f32[2,1152]{1,0:T(2,128)} %bitcast.9, bf16[8,128,1152]{2,1,0:T(8,128)(2,1)} %bitcast.5, bf16[8,128,1152]{2,1,0:T(8,128)(2,1)} %bitcast.6, bf16[36,1728]{1,0:T(8,128)(2,1)} %w1_ref.1, ...), custom_call_target="tpu_custom_call" | custom-call | tf_op jit(solution)/shard_map/block/pallas_call | solution.py:574
  121.7 0.0 copy-start
  121.7 3.3 %copy.14 = bf16[1,8,128,1152]{3,2,1,0:T(8,128)(2,1)} copy(bf16[1,8,128,1152]{3,2,1,0:T(8,128)(2,1)} %bitcast.7) | data formatting | bytes 4718592
  124.9 0.0 copy-done
  124.9 0.6 copy.15
Async XLA Ops:
  121.7 3.3 %copy-start = (f32[36,72]{1,0:T(8,128)S(1)}, f32[36,72]{1,0:T(8,128)}, u32[]{:S(2)}) copy-start(f32[36,72]{1,0:T(8,128)} %get-tuple-element.9) | copy-start | bytes 31108

commit v4 on v3

--- a/solution.py
+++ b/solution.py
@@ -48,7 +48,7 @@
     return jnp.concatenate([top, low], axis=0).astype(BF)
 
 
-STEPS = (
+PLAIN = (
     ((), ("z1p", "z1q", "upp0", "dnp0", "upq0", "dnq0")),
     (("z1p",), ("z2p", "upp1", "dnp1")),
     (("z1q",), ("z2q", "upq1", "dnq1")),
@@ -69,13 +69,52 @@
     (("farp2", "farq2"), ("s2",)),
     (("farp3", "farq3"), ("s3",)),
 )
-
-
-def gather_plan(full, ssem, rsem):
+MIXED = (
+    ((), ("z1p", "z1q", "upp0", "dnp0", "by1u", "by1d", "by2", "upq0", "dnq0", "bz10")),
+    (("z1p",), ("z2p", "upp1", "dnp1")),
+    (("upp0", "dnp0"), ("farp0",)),
+    (("z1q",), ("z2q", "upq1", "dnq1")),
+    (("by1u", "by1d"), ("bz11", "bz12")),
+    (("bz10",), ("bz20",)),
+    (("z2p",), ("z3p", "upp2", "dnp2")),
+    (("z2q",), ("z3q", "upq2", "dnq2")),
+    (("by2",), ("bz13",)),
+    (("upq0", "dnq0"), ("farq0",)),
+    (("bz11",), ("bz21",)),
+    (("upp1", "dnp1"), ("farp1",)),
+    (("bz20",), ("bz30",)),
+    (("bz12",), ("bz22",)),
+    (("upq1", "dnq1"), ("farq1",)),
+    (("z3p",), ("upp3", "dnp3")),
+    (("z3q",), ("upq3", "dnq3")),
+    (("farp0", "farq0"), ("s0",)),
+    (("bz21",), ("bz31",)),
+    (("bz13",), ("bz23",)),
+    (("upp2", "dnp2"), ("farp2",)),
+    (("bz22",), ("bz32",)),
+    (("upq2", "dnq2"), ("farq2",)),
+    (("bz30",), ("bz40",)),
+    (("farp1", "farq1"), ("s1",)),
+    (("bz31",), ("bz41",)),
+    (("upp3", "dnp3"), ("farp3",)),
+    (("bz23",), ("bz33",)),
+    (("upq3", "dnq3"), ("farq3",)),
+    (("bz32",), ("bz42",)),
+    (("farp2", "farq2"), ("s2",)),
+    (("bz40",), ("r0",)),
+    (("bz41",), ("r1",)),
+    (("bz33",), ("bz43",)),
+    (("bz42",), ("r2",)),
+    (("farp3", "farq3"), ("s3",)),
+    (("bz43",), ("r3",)),
+)
+
+
+def gather_plan(full, ssem, rsem, split, order):
     grp, sp = lax.axis_index("grp"), lax.axis_index("sp")
     h, y, c = grp // 8, (grp // 2) % 4, grp % 2
     low = sp % 2
-    up, down = lax.rem(y + 1, 4), lax.rem(y + 3, 4)
+    up, down, far = lax.rem(y + 1, 4), lax.rem(y + 3, 4), lax.rem(y + 2, 4)
     hx = lax.rem(h + 3 + 2 * low, 4)
     hp = lax.rem(h + 5 - 2 * low, 4)
     hf = lax.rem(h + 2, 4)
@@ -91,7 +130,7 @@
     def add(name, where, who):
         table[name] = (len(table), where, who)
 
-    for stream, cols in (("p", pl.ds(0, PACK // 2)), ("q", pl.ds(PACK // 2, PACK // 2))):
+    for stream, cols in (("p", pl.ds(0, split // 2)), ("q", pl.ds(split // 2, split // 2))):
         add("z1" + stream, (h, y, c, al, cols), cross)
         add("z2" + stream, (hx, y, c, al, cols), pair)
         add("z3" + stream, (hp, y, c, al, cols), cross)
@@ -103,7 +142,24 @@
             else:
                 add(f"farq{k}", (hs[k], up, c, al, cols), y_down)
     for k in range(4):
-        add(f"s{k}", (hs[k], al, c), sibling)
+        add(f"s{k}", (hs[k], al, c, al, pl.ds(0, split)), sibling)
+    if split < PACK:
+        rest = PACK - split
+        cols = pl.ds(split, rest)
+        ys = (y, up, down, far)
+
+        def part(which):
+            return pl.ds(pl.multiple_of(split + which * (rest // 2), 128), rest // 2)
+
+        add("by1u", (h, y, c, al, cols), y_up)
+        add("by1d", (h, y, c, al, cols), y_down)
+        add("by2", (h, y, c, al, cols), ((h * 4 + far) * 2 + c, sp))
+        for k in range(4):
+            add(f"bz1{k}", (h, ys[k], c, al, cols), cross)
+            add(f"bz2{k}", (hx, ys[k], c, al, cols), pair)
+            add(f"bz3{k}", (hp, ys[k], c, al, part(1 - low)), cross)
+            add(f"bz4{k}", (hf, ys[k], c, al, part(low)), pair)
+            add(f"r{k}", (al, ys[k], c, al, cols), sibling)
 
     def copy(name):
         i, where, who = table[name]
@@ -123,14 +179,20 @@
         copy(f"s{k}").wait_recv()
         return hs[k]
 
+    def settle_rest():
+        for k in range(4):
+            copy(f"r{k}").wait_recv()
+
     def drain():
         for name in table:
             copy(name).wait_send()
 
-    return [step(*both) for both in STEPS], settle, drain, (h, y, c), cross
-
-
-COPIES = 34
+    settled = (settle, settle_rest if split < PACK else None, hs)
+    return [step(*both) for both in order], settled, drain, (h, y, c), cross
+
+
+COPIES = 57
+SPLIT = 1024
 
 
 def iota(shape, dim):
@@ -141,7 +203,7 @@
     return condition.astype(F32).astype(BF)
 
 
-def unpack(full, settle, wq, wo):
+def unpack(full, settled, wq, wo):
     col, row = iota((144, 192), 1), iota((144, 192), 0)
     of, at = col // 48, col % 48
     top = picks((at < 36) & (36 * of + at == row))
@@ -151,29 +213,50 @@
     left = picks((at >= 0) & (at < 6) & (18 * of + 12 + at == row))
     right = picks((at >= 6) & (18 * of + 6 + at == row))
     keep = iota((144, 128), 1) < 64
-
-    wo[INNER:, :] = jnp.zeros((PAD - INNER, WIDTH), BF)
-    for k in range(4):
-        h = settle(k)
-        outs = []
+    settle, settle_rest, hs = settled
+
+    def block(h, i, first, last):
+        return full[h, 2 * i : 2 * i + 2, :, :, first:last].reshape(192, last - first)
+
+    def rows_of(h, i):
+        return pl.ds(pl.multiple_of((2 * h + i) * 144, 16), 144)
+
+    def low_columns(h):
         for i in range(2):
-            block = full[h, 2 * i : 2 * i + 2].reshape(192, PACK)
-            got = jnp.dot(top, block, preferred_element_type=F32)
-            rows = pl.ds(pl.multiple_of((2 * h + i) * 144, 16), 144)
+            rows = rows_of(h, i)
+            got = jnp.dot(top, block(h, i, 0, SPLIT), preferred_element_type=F32)
             mixed = got[:, 512:640]
             turned = jnp.concatenate([mixed[:, 64:], mixed[:, :64]], axis=1)
             wq[rows, 0:512] = got[:, 0:512].astype(BF)
             wq[rows, 512:640] = jnp.where(keep, mixed, 0.0).astype(BF)
-            wq[rows, 640:1152] = got[:, 640:1152].astype(BF)
+            wq[rows, 640:SPLIT] = got[:, 640:SPLIT].astype(BF)
             wq[rows, 1152:1280] = jnp.where(keep, turned, 0.0).astype(BF)
-            wq[rows, 1280:1920] = got[:, 1152:1792].astype(BF)
-            whole = jnp.dot(main, block[:, :WIDTH], preferred_element_type=F32)
-            side = block[:, WIDTH:]
+
+    def high_columns(h):
+        outs = []
+        for i in range(2):
+            rows, packed = rows_of(h, i), block(h, i, 0, PACK)
+            got = jnp.dot(top, packed[:, SPLIT:], preferred_element_type=F32)
+            wq[rows, SPLIT:1152] = got[:, : 1152 - SPLIT].astype(BF)
+            wq[rows, 1280:1920] = got[:, 1152 - SPLIT :].astype(BF)
+            whole = jnp.dot(main, packed[:, :WIDTH], preferred_element_type=F32)
+            side = packed[:, WIDTH:]
             one = jnp.dot(left, side, preferred_element_type=F32)
             two = jnp.dot(right, side, preferred_element_type=F32)
             blank = jnp.zeros((72, 512), F32)
             outs.append(whole + jnp.concatenate([one, blank], axis=1) + jnp.concatenate([blank, two], axis=1))
         wo[pl.ds(pl.multiple_of(144 * h, 16), 144), :] = jnp.concatenate(outs, axis=0).astype(BF)
+
+    wo[INNER:, :] = jnp.zeros((PAD - INNER, WIDTH), BF)
+    for k in range(4):
+        settle(k)
+        low_columns(hs[k])
+        if settle_rest is None:
+            high_columns(hs[k])
+    if settle_rest is not None:
+        settle_rest()
+        for k in range(4):
+            high_columns(hs[k])
 
 
 def modulated(x, offsets, shift_row, scale_row):
@@ -276,8 +359,8 @@
         return remote(
             ap.at[lax.rem(to, SENDERS), pairs], attp.at[sp, pairs], back_s.at[i, d], back_r.at[i, d], (grp, to))
 
-    steps_s, settle_s, drain_s, here, cross = gather_plan(full_s, gs_s, gr_s)
-    steps_t, settle_t, drain_t, _, _ = gather_plan(full_t, gs_t, gr_t)
+    steps_s, settled_s, drain_s, here, cross = gather_plan(full_s, gs_s, gr_s, SPLIT, MIXED)
+    steps_t, settled_t, drain_t, _, _ = gather_plan(full_t, gs_t, gr_t, PACK, PLAIN)
     loads = [
         pltpu.make_async_copy(hidden_ref, hid, load_sem.at[0]),
         pltpu.make_async_copy(cot_in_ref, cot, load_sem.at[1]),
@@ -316,17 +399,20 @@
             def _(i=i):
                 steps_s[1 + i]()
 
-        @pl.when((f == 1) & busy)
-        def _():
-            for d in (3, 5, 1, 7):
-                early(d).start()
-
-    for run in steps_s[9:17]:
+    for run in steps_s[9:22]:
+        run()
+
+    @pl.when(busy)
+    def _():
+        for d in (3, 5, 1, 7):
+            early(d).start()
+
+    for run in steps_s[22:29]:
         run()
     steps_t[0]()
-    for run in steps_s[17:]:
+    for run in steps_s[29:]:
         run()
-    unpack(full_s, settle_s, wq, wo_s)
+    unpack(full_s, settled_s, wq, wo_s)
 
     rest = steps_t[1:]
 
@@ -346,10 +432,10 @@
         for n in range(batches):
             @pl.when(i == n)
             def _(n=n):
-                for run in rest[2 * n : 2 * n + 2]:
+                for run in rest[(0, 5, 8, 10)[n] : (5, 8, 10, 12)[n]]:
                     run()
 
-    rest = rest[2 * batches :]
+    rest = rest[12:]
 
     for d in range(1, 8):
         @if_sends(d)
@@ -362,6 +448,12 @@
 
     @pl.loop(0, batches)
     def _(i):
+        for n in range(batches):
+            @pl.when(i == n)
+            def _(n=n):
+                for run in rest[2 * n : 2 * n + 2]:
+                    run()
+
         for d in range(1, 8):
             @if_sends(d)
             def _(d=d):
@@ -378,12 +470,6 @@
         normed = modulated(middle.astype(BF).astype(F32), offsets, 2, 3)
         x_in[:, frames] = normed.reshape(SENDERS, BATCH, OWN, WIDTH)
 
-        for n in range(batches):
-            @pl.when(i == n)
-            def _(n=n):
-                for run in rest[n : n + 1]:
-                    run()
-
     order = shuffle(False)
 
     @pl.loop(0, SENDERS)
@@ -391,9 +477,7 @@
         got = jnp.dot(order, x_in[s].reshape(128, WIDTH), preferred_element_type=F32).astype(BF)
         xp[:, s] = got.reshape(GROUPS, 16, WIDTH)
 
-    for run in rest[batches:]:
-        run()
-    unpack(full_t, settle_t, wq, wo_t)
+    unpack(full_t, settled_t, wq, wo_t)
 
     key, row = iota((rows, PIX), 1), iota((rows, PIX), 0)
     frame = (key // 16) * 8 + key % 8

time: 126 us -> 144 us (1.14)
  Pallas kernels: 120 us -> 138 us
    pallas_call x1, Pallas kernels: 120 us -> 138 us  [on_device(): pl.pallas_call(block_kernel, out_shape=(jax.ShapeDtypeStruct(frames, BF),...]
where the time goes in v4:
time: 144 us
  Pallas kernels  138 us (96%)
  local copies, waits for them, and re-layouts  3.88 us (3%)
    pallas_call x1, Pallas kernels, on_device(): pl.pallas_call(block_kernel, out_shape=(jax.ShapeDtypeStruct(frames, BF),...  138 us
    unnamed x4, local copies, waits for them, and re-layouts  3.88 us

profile of v4, /device:TPU:7, one launch (start us, length us, event | category | flops | bytes accessed | tf_op | source)
XLA Modules:
  0.0 143.6 jit_solution(4178026373390648384)
XLA Ops:
  1.3 138.4 %block.1 = (bf16[8,128,1152]{2,1,0:T(8,128)(2,1)}, f32[36,72]{1,0:T(8,128)}) custom-call(s32[1]{0:T(128)S(6)} %copy.13.total_ref, f32[4,1152]{1,0:T(4,128)} %bitcast.8, f32[2,1152]{1,0:T(2,128)} %bitcast.9, bf16[8,128,1152]{2,1,0:T(8,128)(2,1)} %bitcast.5, bf16[8,128,1152]{2,1,0:T(8,128)(2,1)} %bitcast.6, bf16[36,1728]{1,0:T(8,128)(2,1)} %w1_ref.1, ...), custom_call_target="tpu_custom_call" | custom-call | tf_op jit(solution)/shard_map/block/pallas_call | solution.py:658
  139.7 0.0 copy-start
  139.7 3.3 %copy.14 = bf16[1,8,128,1152]{3,2,1,0:T(8,128)(2,1)} copy(bf16[1,8,128,1152]{3,2,1,0:T(8,128)(2,1)} %bitcast.7) | data formatting | bytes 4718592
  143.0 0.0 copy-done
  143.0 0.6 copy.15
Async XLA Ops:
  139.7 3.3 %copy-start = (f32[36,72]{1,0:T(8,128)S(1)}, f32[36,72]{1,0:T(8,128)}, u32[]{:S(2)}) copy-start(f32[36,72]{1,0:T(8,128)} %get-tuple-element.9) | copy-start | bytes 31108

commit v5 on v3

--- a/solution.py
+++ b/solution.py
@@ -28,13 +28,6 @@
 BIG = 56 * 1024 * 1024
 
 
-def greet(partners):
-    barrier = pltpu.get_barrier_semaphore()
-    for who in partners:
-        pl.semaphore_signal(barrier, inc=1, device_id=who, device_id_type=MESH)
-    pl.semaphore_wait(barrier, len(partners))
-
-
 def pack(qkv_ref, out_ref):
     qkv, out = qkv_ref[...].astype(F32), out_ref[...].astype(F32)
     k, v = qkv[:, INNER : 2 * INNER], qkv[:, 2 * INNER :]
@@ -49,7 +42,8 @@
 
 
 STEPS = (
-    ((), ("z1p", "z1q", "upp0", "dnp0", "upq0", "dnq0")),
+    ((), ("z1p", "z1q")),
+    ((), ("upp0", "dnp0", "upq0", "dnq0")),
     (("z1p",), ("z2p", "upp1", "dnp1")),
     (("z1q",), ("z2q", "upq1", "dnq1")),
     (("upp0", "dnp0"), ("farp0",)),
@@ -127,7 +121,7 @@
         for name in table:
             copy(name).wait_send()
 
-    return [step(*both) for both in STEPS], settle, drain, (h, y, c), cross
+    return [step(*both) for both in STEPS], settle, drain, (h, y, c), [sibling, y_up, y_down, cross]
 
 
 COPIES = 34
@@ -227,7 +221,7 @@
     total_ref, shift_ref, gate_ref, hidden_ref, cot_in_ref, w1_ref, w2_ref, w3_ref, w4_ref,
     out_ref, grad_ref,
     full_s, full_t, wq, wo_s, wo_t, hid, nrm, mid, cot, qkv, att_s, x_in, a_in, xp, qkv_t, ap, attp, att,
-    g_part, r0, red, r1, flipped, buf, r2,
+    scp, acc, g_part, r0, red, r1, flipped, buf, r2,
     gs_s, gr_s, gs_t, gr_t, load_sem, early_s, early_r, there_s, there_r, there_l, back_s, back_r,
     s0, t0, s1, t1, s2, t2, out_sem,
 ):
@@ -258,9 +252,10 @@
             src_ref=src, dst_ref=dst, send_sem=send_sem, recv_sem=recv_sem,
             device_id=who, device_id_type=MESH)
 
-    def early(d):
-        to = from_me(d)
-        return remote(hidden_ref.at[:, pixels(to), :], x_in.at[slot], early_s.at[d], early_r.at[d], (grp, to))
+    def early(i, d):
+        to, frames = from_me(d), pl.ds(BATCH * i, BATCH)
+        return remote(
+            hidden_ref.at[frames, pixels(to), :], x_in.at[slot, frames], early_s.at[i, d], early_r.at[i, d], (grp, to))
 
     def there(i, d):
         to, frames = from_me(d), pl.ds(BATCH * i, BATCH)
@@ -276,7 +271,7 @@
         return remote(
             ap.at[lax.rem(to, SENDERS), pairs], attp.at[sp, pairs], back_s.at[i, d], back_r.at[i, d], (grp, to))
 
-    steps_s, settle_s, drain_s, here, cross = gather_plan(full_s, gs_s, gr_s)
+    steps_s, settle_s, drain_s, here, neighbours = gather_plan(full_s, gs_s, gr_s)
     steps_t, settle_t, drain_t, _, _ = gather_plan(full_t, gs_t, gr_t)
     loads = [
         pltpu.make_async_copy(hidden_ref, hid, load_sem.at[0]),
@@ -290,20 +285,25 @@
     def _():
         loads[2].start()
 
+    partners = neighbours + [(grp, from_me(d)) for d in range(1, 8)]
+    barrier = pltpu.get_barrier_semaphore()
+    for who in partners:
+        pl.semaphore_signal(barrier, inc=1, device_id=who, device_id_type=MESH)
     full_s[here] = pack(w1_ref, w2_ref)
-    full_t[here] = pack(w3_ref, w4_ref)
-    greet_all = [(lax.rem(grp + d, 32), sp) for d in range(1, 32)]
-    greet_all += [(grp, from_me(d)) for d in range(1, 8)] + [cross]
-    greet(greet_all)
+    pl.semaphore_wait(barrier, len(partners))
     steps_s[0]()
+    steps_s[1]()
 
     @pl.when(busy)
     def _():
-        for d in (4, 2, 6):
-            early(d).start()
-
+        for d in (3, 5, 1, 7):
+            early(0, d).start()
+        for i in range(batches):
+            for d in (4, 2, 6):
+                early(i, d).start()
+
+    full_t[here] = pack(w3_ref, w4_ref)
     loads[0].wait()
-    loads[1].wait()
 
     @pl.loop(0, SLOTS)
     def _(f):
@@ -314,21 +314,26 @@
         for i in range(SLOTS):
             @pl.when(f == i)
             def _(i=i):
-                steps_s[1 + i]()
-
-        @pl.when((f == 1) & busy)
+                steps_s[2 + i]()
+
+        @pl.when((f == 5) & busy)
         def _():
-            for d in (3, 5, 1, 7):
-                early(d).start()
-
-    for run in steps_s[9:17]:
+            @pl.loop(1, batches)
+            def _(i):
+                for d in (3, 5, 1, 7):
+                    early(i, d).start()
+
+    for run in steps_s[10:12]:
         run()
     steps_t[0]()
-    for run in steps_s[17:]:
+    for run in steps_s[12:18]:
+        run()
+    steps_t[1]()
+    for run in steps_s[18:]:
         run()
     unpack(full_s, settle_s, wq, wo_s)
 
-    rest = steps_t[1:]
+    rest = steps_t[2:]
 
     @pl.loop(0, batches)
     def _(i):
@@ -346,15 +351,11 @@
         for n in range(batches):
             @pl.when(i == n)
             def _(n=n):
-                for run in rest[2 * n : 2 * n + 2]:
+                for run in rest[(0, 5, 8, 10)[n] : (5, 8, 10, 12)[n]]:
                     run()
 
-    rest = rest[2 * batches :]
-
-    for d in range(1, 8):
-        @if_sends(d)
-        def _(d=d):
-            early(d).wait_recv()
+    rest = rest[12:]
+    loads[1].wait()
 
     @pl.when(busy)
     def _():
@@ -362,9 +363,16 @@
 
     @pl.loop(0, batches)
     def _(i):
+        for n in range(batches):
+            @pl.when(i == n)
+            def _(n=n):
+                for run in rest[2 * n : 2 * n + 2]:
+                    run()
+
         for d in range(1, 8):
             @if_sends(d)
             def _(d=d):
+                early(i, d).wait_recv()
                 there(i, d).wait_recv()
 
         @pl.when(busy)
@@ -378,12 +386,6 @@
         normed = modulated(middle.astype(BF).astype(F32), offsets, 2, 3)
         x_in[:, frames] = normed.reshape(SENDERS, BATCH, OWN, WIDTH)
 
-        for n in range(batches):
-            @pl.when(i == n)
-            def _(n=n):
-                for run in rest[n : n + 1]:
-                    run()
-
     order = shuffle(False)
 
     @pl.loop(0, SENDERS)
@@ -391,8 +393,6 @@
         got = jnp.dot(order, x_in[s].reshape(128, WIDTH), preferred_element_type=F32).astype(BF)
         xp[:, s] = got.reshape(GROUPS, 16, WIDTH)
 
-    for run in rest[batches:]:
-        run()
     unpack(full_t, settle_t, wq, wo_t)
 
     key, row = iota((rows, PIX), 1), iota((rows, PIX), 0)
@@ -437,21 +437,33 @@
             mid[f] = (hid[f].astype(F32) + gate_ref[0:1, :] * branch).astype(BF)
             nrm[f] = jnp.where(kept, gate_ref[1:2, :] * cot[f].astype(F32), 0.0).astype(BF)
 
-        unorder = shuffle(True)
-        for i in range(GROUPS // 2):
+        @pl.loop(0, 8)
+        def _(t):
+            got = jnp.dot(order, nrm[:, pixels(t), :].reshape(128, WIDTH), preferred_element_type=F32)
+            scp[t] = got.astype(BF).reshape(GROUPS, 16, WIDTH)
+
+        def product(i, cols):
+            pairs = pl.ds(2 * i, 2)
+            return lax.dot_general(
+                attp[:, pairs].reshape(2 * PIX, PAD), scp[:, pairs, :, cols].reshape(2 * PIX, 384),
+                (((0,), (0,)), ((), ())), preferred_element_type=F32)
+
+        acc[...] = jnp.zeros_like(acc)
+
+        @pl.loop(0, GROUPS // 2 - 1)
+        def _(i):
             for d in range(1, 8):
                 back(i, d).wait_recv()
-
-        @pl.loop(0, 8)
-        def _(t):
-            got = jnp.dot(unorder, attp[t].reshape(128, PAD), preferred_element_type=F32).astype(BF)
-            att[:, pixels(t), :] = got.reshape(SLOTS, OWN, PAD)
+            for n in range(3):
+                cols = slice(384 * n, 384 * n + 384)
+                acc[:, cols] += product(i, cols)
+
+        for d in range(1, 8):
+            back(GROUPS // 2 - 1, d).wait_recv()
 
         def gradient(n):
             cols = slice(384 * n, 384 * n + 384)
-            got = lax.dot_general(
-                att[...].reshape(SLOTS * PIX, PAD), nrm[:, :, cols].reshape(SLOTS * PIX, 384),
-                (((0,), (0,)), ((), ())), preferred_element_type=F32) * (1.0 / PIX)
+            got = (acc[:, cols] + product(GROUPS // 2 - 1, cols)) * (1.0 / PIX)
             for t in range(8):
                 part = jnp.concatenate([got[72 * t : 72 * t + 72], jnp.zeros((8, 384), F32)], axis=0)
                 g_part[t // 2, t % 2, :, cols] = part.astype(BF)
@@ -477,6 +489,12 @@
         gradient(2)
         pass_on(1)
         pass_on(2)
+        unorder = shuffle(True)
+
+        @pl.loop(0, 8)
+        def _(t):
+            got = jnp.dot(unorder, attp[t].reshape(128, PAD), preferred_element_type=F32).astype(BF)
+            att[:, pixels(t), :] = got.reshape(SLOTS, OWN, PAD)
 
         @pl.loop(0, SLOTS)
         def _(f):
@@ -545,8 +563,8 @@
                     step1(n, i).wait_send()
 
         for d in range(1, 8):
-            early(d).wait_send()
             for i in range(batches):
+                early(i, d).wait_send()
                 there(i, d).wait_send()
 
     for i in range(GROUPS // 2):
@@ -592,6 +610,8 @@
             pltpu.VMEM((SENDERS, GROUPS, 16, PAD), BF),
             pltpu.VMEM((8, GROUPS, 16, PAD), BF),
             pltpu.VMEM((SLOTS, PIX, PAD), BF),
+            pltpu.VMEM((8, GROUPS, 16, WIDTH), BF),
+            pltpu.VMEM((PAD, WIDTH), F32),
             pltpu.VMEM((4, 2, 80, WIDTH), BF),
             pltpu.VMEM((4, 80, WIDTH), BF),
             pltpu.VMEM((4, 80, WIDTH), BF),
@@ -600,7 +620,7 @@
             pltpu.VMEM((32, 48, 128), BF),
             pltpu.VMEM((16, 48, 128), BF),
             dma((COPIES,)), dma((COPIES,)), dma((COPIES,)), dma((COPIES,)),
-            dma((3,)), dma((8,)), dma((8,)),
+            dma((3,)), dma((4, 8)), dma((4, 8)),
             dma((4, 8)), dma((4, 8)), dma((4,)),
             dma((4, 8)), dma((4, 8)),
             dma((3,)), dma((3,)), dma((3, 4)), dma((3, SENDERS)), dma((32,)), dma((32,)), dma,

time: 126 us -> 121 us (0.960)
  Pallas kernels: 120 us -> 115 us
    pallas_call x1, Pallas kernels: 120 us -> 115 us  [on_device(): pl.pallas_call(block_kernel, out_shape=(jax.ShapeDtypeStruct(frames, BF),...]
where the time goes in v5:
time: 121 us; the launch traced here: 120 us
  Pallas kernels  115 us (95%)
  local copies, waits for them, and re-layouts  3.88 us (3%)
  between operations  1.3 us (1%)
    pallas_call x1, Pallas kernels, on_device(): pl.pallas_call(block_kernel, out_shape=(jax.ShapeDtypeStruct(frames, BF),...  115 us
    unnamed x4, local copies, waits for them, and re-layouts  3.88 us

profile of v5, /device:TPU:7, one launch (start us, length us, event | category | flops | bytes accessed | tf_op | source)
XLA Modules:
  0.0 120.2 jit_solution(9193977643928259641)
XLA Ops:
  1.3 115.0 %block.1 = (bf16[8,128,1152]{2,1,0:T(8,128)(2,1)}, f32[36,72]{1,0:T(8,128)}) custom-call(s32[1]{0:T(128)S(6)} %copy.13.total_ref, f32[4,1152]{1,0:T(4,128)} %bitcast.8, f32[2,1152]{1,0:T(2,128)} %bitcast.9, bf16[8,128,1152]{2,1,0:T(8,128)(2,1)} %bitcast.5, bf16[8,128,1152]{2,1,0:T(8,128)(2,1)} %bitcast.6, bf16[36,1728]{1,0:T(8,128)(2,1)} %w1_ref.1, ...), custom_call_target="tpu_custom_call" | custom-call | tf_op jit(solution)/shard_map/block/pallas_call | solution.py:592
  116.3 0.0 copy-start
  116.3 3.3 %copy.14 = bf16[1,8,128,1152]{3,2,1,0:T(8,128)(2,1)} copy(bf16[1,8,128,1152]{3,2,1,0:T(8,128)(2,1)} %bitcast.7) | data formatting | bytes 4718592
  119.6 0.0 copy-done
  119.6 0.6 copy.15
Async XLA Ops:
  116.3 3.3 %copy-start = (f32[36,72]{1,0:T(8,128)S(1)}, f32[36,72]{1,0:T(8,128)}, u32[]{:S(2)}) copy-start(f32[36,72]{1,0:T(8,128)} %get-tuple-element.9) | copy-start | bytes 31108

commit v6 on v5

--- a/solution.py
+++ b/solution.py
@@ -63,9 +63,31 @@
     (("farp2", "farq2"), ("s2",)),
     (("farp3", "farq3"), ("s3",)),
 )
-
-
-def gather_plan(full, ssem, rsem):
+LATER = (
+    ((), ("z1p", "z1q")),
+    (("z1p",), ("z2p",)),
+    (("z1q",), ("z2q",)),
+    ((), ("upp0", "dnp0", "upq0", "dnq0", "upp1", "dnp1", "upq1", "dnq1")),
+    (("z2p",), ("z3p", "upp2", "dnp2")),
+    (("z2q",), ("z3q", "upq2", "dnq2")),
+    (("upp0", "dnp0"), ("farp0",)),
+    (("upq0", "dnq0"), ("farq0",)),
+    (("upp1", "dnp1"), ("farp1",)),
+    (("upq1", "dnq1"), ("farq1",)),
+    (("farp0", "farq0"), ("s0",)),
+    (("z3p",), ("upp3", "dnp3")),
+    (("z3q",), ("upq3", "dnq3")),
+    (("upp2", "dnp2"), ("farp2",)),
+    (("upq2", "dnq2"), ("farq2",)),
+    (("farp1", "farq1"), ("s1",)),
+    (("farp2", "farq2"), ("s2",)),
+    (("upp3", "dnp3"), ("farp3",)),
+    (("upq3", "dnq3"), ("farq3",)),
+    (("farp3", "farq3"), ("s3",)),
+)
+
+
+def gather_plan(full, ssem, rsem, order):
     grp, sp = lax.axis_index("grp"), lax.axis_index("sp")
     h, y, c = grp // 8, (grp // 2) % 4, grp % 2
     low = sp % 2
@@ -121,7 +143,7 @@
         for name in table:
             copy(name).wait_send()
 
-    return [step(*both) for both in STEPS], settle, drain, (h, y, c), [sibling, y_up, y_down, cross]
+    return [step(*both) for both in order], settle, drain, (h, y, c), [sibling, y_up, y_down, cross]
 
 
 COPIES = 34
@@ -266,13 +288,13 @@
         frames = pl.ds(BATCH * i, BATCH)
         return pltpu.make_async_copy(att_s.at[frames, pixels(sp), :], a_in.at[slot, frames], there_l.at[i])
 
-    def back(i, d):
-        to, pairs = from_me(d), pl.ds(2 * i, 2)
+    def back(g, d):
+        to = from_me(d)
         return remote(
-            ap.at[lax.rem(to, SENDERS), pairs], attp.at[sp, pairs], back_s.at[i, d], back_r.at[i, d], (grp, to))
-
-    steps_s, settle_s, drain_s, here, neighbours = gather_plan(full_s, gs_s, gr_s)
-    steps_t, settle_t, drain_t, _, _ = gather_plan(full_t, gs_t, gr_t)
+            ap.at[lax.rem(to, SENDERS), g], attp.at[sp, g], back_s.at[g, d], back_r.at[g, d], (grp, to))
+
+    steps_s, settle_s, drain_s, here, neighbours = gather_plan(full_s, gs_s, gr_s, STEPS)
+    steps_t, settle_t, drain_t, _, _ = gather_plan(full_t, gs_t, gr_t, LATER)
     loads = [
         pltpu.make_async_copy(hidden_ref, hid, load_sem.at[0]),
         pltpu.make_async_copy(cot_in_ref, cot, load_sem.at[1]),
@@ -323,17 +345,13 @@
                 for d in (3, 5, 1, 7):
                     early(i, d).start()
 
-    for run in steps_s[10:12]:
+    for run in steps_s[10:12] + steps_t[0:1] + steps_s[12:16] + steps_t[1:3] + steps_s[16:18] + steps_t[3:4]:
         run()
-    steps_t[0]()
-    for run in steps_s[12:18]:
-        run()
-    steps_t[1]()
     for run in steps_s[18:]:
         run()
     unpack(full_s, settle_s, wq, wo_s)
-
-    rest = steps_t[2:]
+    for run in steps_t[4:8]:
+        run()
 
     @pl.loop(0, batches)
     def _(i):
@@ -351,10 +369,9 @@
         for n in range(batches):
             @pl.when(i == n)
             def _(n=n):
-                for run in rest[(0, 5, 8, 10)[n] : (5, 8, 10, 12)[n]]:
+                for run in steps_t[(8, 11, 13, 16)[n] : (11, 13, 16, 17)[n]]:
                     run()
 
-    rest = rest[12:]
     loads[1].wait()
 
     @pl.when(busy)
@@ -366,8 +383,17 @@
         for n in range(batches):
             @pl.when(i == n)
             def _(n=n):
-                for run in rest[2 * n : 2 * n + 2]:
+                for run in steps_t[(17, 19, 20, 20)[n] : (19, 20, 20, 20)[n]]:
                     run()
+
+        @pl.when(busy)
+        def _():
+            for u in range(BATCH):
+                f = BATCH * i + u
+                kept = sp * SLOTS + f < total
+                branch = jnp.dot(att_s[f], wo_s[...], preferred_element_type=F32)
+                mid[f] = (hid[f].astype(F32) + gate_ref[0:1, :] * branch).astype(BF)
+                nrm[f] = jnp.where(kept, gate_ref[1:2, :] * cot[f].astype(F32), 0.0).astype(BF)
 
         for d in range(1, 8):
             @if_sends(d)
@@ -392,6 +418,15 @@
     def _(s):
         got = jnp.dot(order, x_in[s].reshape(128, WIDTH), preferred_element_type=F32).astype(BF)
         xp[:, s] = got.reshape(GROUPS, 16, WIDTH)
+
+    @pl.when(busy)
+    def _():
+        @pl.loop(0, 8)
+        def _(t):
+            got = jnp.dot(order, nrm[:, pixels(t), :].reshape(128, WIDTH), preferred_element_type=F32)
+            scp[t] = got.astype(BF).reshape(GROUPS, 16, WIDTH)
+
+        acc[...] = jnp.zeros_like(acc)
 
     unpack(full_t, settle_t, wq, wo_t)
 
@@ -406,10 +441,10 @@
         for u in range(2):
             mixed = attention(lambda first: qkv_t[u, :, first : first + 256], rows, valid)
             ap[:, 2 * i + u] = mixed.reshape(SENDERS, 16, PAD)
-        for d in (4, 3, 5, 2, 6, 1, 7):
-            @if_gets(d)
-            def _(d=d):
-                back(i, d).start()
+            for d in (4, 3, 5, 2, 6, 1, 7):
+                @if_gets(d)
+                def _(d=d, u=u):
+                    back(2 * i + u, d).start()
 
         @pl.when(busy)
         def _():
@@ -430,36 +465,24 @@
 
     @pl.when(busy)
     def _():
-        @pl.loop(0, SLOTS)
-        def _(f):
-            kept = sp * SLOTS + f < total
-            branch = jnp.dot(att_s[f], wo_s[...], preferred_element_type=F32)
-            mid[f] = (hid[f].astype(F32) + gate_ref[0:1, :] * branch).astype(BF)
-            nrm[f] = jnp.where(kept, gate_ref[1:2, :] * cot[f].astype(F32), 0.0).astype(BF)
-
-        @pl.loop(0, 8)
-        def _(t):
-            got = jnp.dot(order, nrm[:, pixels(t), :].reshape(128, WIDTH), preferred_element_type=F32)
-            scp[t] = got.astype(BF).reshape(GROUPS, 16, WIDTH)
-
         def product(i, cols):
             pairs = pl.ds(2 * i, 2)
             return lax.dot_general(
                 attp[:, pairs].reshape(2 * PIX, PAD), scp[:, pairs, :, cols].reshape(2 * PIX, 384),
                 (((0,), (0,)), ((), ())), preferred_element_type=F32)
 
-        acc[...] = jnp.zeros_like(acc)
-
         @pl.loop(0, GROUPS // 2 - 1)
         def _(i):
             for d in range(1, 8):
-                back(i, d).wait_recv()
+                back(2 * i, d).wait_recv()
+                back(2 * i + 1, d).wait_recv()
             for n in range(3):
                 cols = slice(384 * n, 384 * n + 384)
                 acc[:, cols] += product(i, cols)
 
         for d in range(1, 8):
-            back(GROUPS // 2 - 1, d).wait_recv()
+            back(GROUPS - 2, d).wait_recv()
+            back(GROUPS - 1, d).wait_recv()
 
         def gradient(n):
             cols = slice(384 * n, 384 * n + 384)
@@ -567,11 +590,11 @@
                 early(i, d).wait_send()
                 there(i, d).wait_send()
 
-    for i in range(GROUPS // 2):
+    for g in range(GROUPS):
         for d in range(1, 8):
             @if_gets(d)
-            def _(d=d, i=i):
-                back(i, d).wait_send()
+            def _(d=d, g=g):
+                back(g, d).wait_send()
 
     result.wait()
 
@@ -622,7 +645,7 @@
             dma((COPIES,)), dma((COPIES,)), dma((COPIES,)), dma((COPIES,)),
             dma((3,)), dma((4, 8)), dma((4, 8)),
             dma((4, 8)), dma((4, 8)), dma((4,)),
-            dma((4, 8)), dma((4, 8)),
+            dma((8, 8)), dma((8, 8)),
             dma((3,)), dma((3,)), dma((3, 4)), dma((3, SENDERS)), dma((32,)), dma((32,)), dma,
         ],
         compiler_params=pltpu.CompilerParams(

time: 121 us -> 123 us (1.017)
  Pallas kernels: 115 us -> 118 us
    pallas_call x1, Pallas kernels: 115 us -> 118 us  [on_device(): pl.pallas_call(block_kernel, out_shape=(jax.ShapeDtypeStruct(frames, BF),...]
where the time goes in v6:
time: 123 us
  Pallas kernels  118 us (96%)
  local copies, waits for them, and re-layouts  3.88 us (3%)
  between operations  1.3 us (1%)
    pallas_call x1, Pallas kernels, on_device(): pl.pallas_call(block_kernel, out_shape=(jax.ShapeDtypeStruct(frames, BF),...  118 us
    unnamed x4, local copies, waits for them, and re-layouts  3.88 us

profile of v6, /device:TPU:7, one launch (start us, length us, event | category | flops | bytes accessed | tf_op | source)
XLA Modules:
  0.0 122.7 jit_solution(7470181303303551486)
XLA Ops:
  1.3 117.5 %block.1 = (bf16[8,128,1152]{2,1,0:T(8,128)(2,1)}, f32[36,72]{1,0:T(8,128)}) custom-call(s32[1]{0:T(128)S(6)} %copy.13.total_ref, f32[4,1152]{1,0:T(4,128)} %bitcast.8, f32[2,1152]{1,0:T(2,128)} %bitcast.9, bf16[8,128,1152]{2,1,0:T(8,128)(2,1)} %bitcast.5, bf16[8,128,1152]{2,1,0:T(8,128)(2,1)} %bitcast.6, bf16[36,1728]{1,0:T(8,128)(2,1)} %w1_ref.1, ...), custom_call_target="tpu_custom_call" | custom-call | tf_op jit(solution)/shard_map/block/pallas_call | solution.py:615
  118.8 0.0 copy-start
  118.8 3.3 %copy.14 = bf16[1,8,128,1152]{3,2,1,0:T(8,128)(2,1)} copy(bf16[1,8,128,1152]{3,2,1,0:T(8,128)(2,1)} %bitcast.7) | data formatting | bytes 4718592
  122.1 0.0 copy-done
  122.1 0.6 copy.15
Async XLA Ops:
  118.8 3.3 %copy-start = (f32[36,72]{1,0:T(8,128)S(1)}, f32[36,72]{1,0:T(8,128)}, u32[]{:S(2)}) copy-start(f32[36,72]{1,0:T(8,128)} %get-tuple-element.9) | copy-start | bytes 31108

commit v7 on v6

--- a/solution.py
+++ b/solution.py
@@ -67,22 +67,21 @@
     ((), ("z1p", "z1q")),
     (("z1p",), ("z2p",)),
     (("z1q",), ("z2q",)),
-    ((), ("upp0", "dnp0", "upq0", "dnq0", "upp1", "dnp1", "upq1", "dnq1")),
-    (("z2p",), ("z3p", "upp2", "dnp2")),
-    (("z2q",), ("z3q", "upq2", "dnq2")),
+    (("z2p",), ("z3p",)),
+    (("z2q",), ("z3q",)),
+    ((), ("upp0", "dnp0", "upq0", "dnq0", "upp1", "dnp1", "upq1", "dnq1", "upp2", "dnp2", "upq2", "dnq2")),
+    (("z3p", "z3q"), ("upp3", "dnp3", "upq3", "dnq3")),
     (("upp0", "dnp0"), ("farp0",)),
     (("upq0", "dnq0"), ("farq0",)),
     (("upp1", "dnp1"), ("farp1",)),
     (("upq1", "dnq1"), ("farq1",)),
     (("farp0", "farq0"), ("s0",)),
-    (("z3p",), ("upp3", "dnp3")),
-    (("z3q",), ("upq3", "dnq3")),
     (("upp2", "dnp2"), ("farp2",)),
     (("upq2", "dnq2"), ("farq2",)),
     (("farp1", "farq1"), ("s1",)),
-    (("farp2", "farq2"), ("s2",)),
     (("upp3", "dnp3"), ("farp3",)),
     (("upq3", "dnq3"), ("farq3",)),
+    (("farp2", "farq2"), ("s2",)),
     (("farp3", "farq3"), ("s3",)),
 )
 
@@ -315,6 +314,8 @@
     pl.semaphore_wait(barrier, len(partners))
     steps_s[0]()
     steps_s[1]()
+    full_t[here] = pack(w3_ref, w4_ref)
+    steps_t[0]()
 
     @pl.when(busy)
     def _():
@@ -324,7 +325,6 @@
             for d in (4, 2, 6):
                 early(i, d).start()
 
-    full_t[here] = pack(w3_ref, w4_ref)
     loads[0].wait()
 
     @pl.loop(0, SLOTS)
@@ -337,6 +337,8 @@
             @pl.when(f == i)
             def _(i=i):
                 steps_s[2 + i]()
+                if i in (4, 5):
+                    steps_t[i - 3]()
 
         @pl.when((f == 5) & busy)
         def _():
@@ -345,12 +347,10 @@
                 for d in (3, 5, 1, 7):
                     early(i, d).start()
 
-    for run in steps_s[10:12] + steps_t[0:1] + steps_s[12:16] + steps_t[1:3] + steps_s[16:18] + steps_t[3:4]:
-        run()
-    for run in steps_s[18:]:
+    for run in steps_s[10:14] + steps_t[3:5] + steps_s[14:18] + steps_t[5:6] + steps_s[18:] + steps_t[6:7]:
         run()
     unpack(full_s, settle_s, wq, wo_s)
-    for run in steps_t[4:8]:
+    for run in steps_t[7:9]:
         run()
 
     @pl.loop(0, batches)
@@ -369,7 +369,7 @@
         for n in range(batches):
             @pl.when(i == n)
             def _(n=n):
-                for run in steps_t[(8, 11, 13, 16)[n] : (11, 13, 16, 17)[n]]:
+                for run in steps_t[(9, 12, 12, 15)[n] : (12, 12, 15, 15)[n]]:
                     run()
 
     loads[1].wait()
@@ -383,7 +383,7 @@
         for n in range(batches):
             @pl.when(i == n)
             def _(n=n):
-                for run in steps_t[(17, 19, 20, 20)[n] : (19, 20, 20, 20)[n]]:
+                for run in steps_t[(15, 18, 19, 19)[n] : (18, 19, 19, 19)[n]]:
                     run()
 
         @pl.when(busy)
@@ -418,15 +418,6 @@
     def _(s):
         got = jnp.dot(order, x_in[s].reshape(128, WIDTH), preferred_element_type=F32).astype(BF)
         xp[:, s] = got.reshape(GROUPS, 16, WIDTH)
-
-    @pl.when(busy)
-    def _():
-        @pl.loop(0, 8)
-        def _(t):
-            got = jnp.dot(order, nrm[:, pixels(t), :].reshape(128, WIDTH), preferred_element_type=F32)
-            scp[t] = got.astype(BF).reshape(GROUPS, 16, WIDTH)
-
-        acc[...] = jnp.zeros_like(acc)
 
     unpack(full_t, settle_t, wq, wo_t)
 
@@ -465,6 +456,13 @@
 
     @pl.when(busy)
     def _():
+        @pl.loop(0, 8)
+        def _(t):
+            got = jnp.dot(order, nrm[:, pixels(t), :].reshape(128, WIDTH), preferred_element_type=F32)
+            scp[t] = got.astype(BF).reshape(GROUPS, 16, WIDTH)
+
+        acc[...] = jnp.zeros_like(acc)
+
         def product(i, cols):
             pairs = pl.ds(2 * i, 2)
             return lax.dot_general(

time: 123 us -> 121 us (0.984)
  Pallas kernels: 118 us -> 116 us
    pallas_call x1, Pallas kernels: 118 us -> 116 us  [on_device(): pl.pallas_call(block_kernel, out_shape=(jax.ShapeDtypeStruct(frames, BF),...]
where the time goes in v7:
time: 121 us
  Pallas kernels  116 us (96%)
  local copies, waits for them, and re-layouts  3.88 us (3%)
  between operations  1.3 us (1%)
    pallas_call x1, Pallas kernels, on_device(): pl.pallas_call(block_kernel, out_shape=(jax.ShapeDtypeStruct(frames, BF),...  116 us
    unnamed x4, local copies, waits for them, and re-layouts  3.88 us

profile of v7, /device:TPU:7, one launch (start us, length us, event | category | flops | bytes accessed | tf_op | source)
XLA Modules:
  0.0 120.8 jit_solution(3175283934844218364)
XLA Ops:
  1.3 115.6 %block.1 = (bf16[8,128,1152]{2,1,0:T(8,128)(2,1)}, f32[36,72]{1,0:T(8,128)}) custom-call(s32[1]{0:T(128)S(6)} %copy.13.total_ref, f32[4,1152]{1,0:T(4,128)} %bitcast.8, f32[2,1152]{1,0:T(2,128)} %bitcast.9, bf16[8,128,1152]{2,1,0:T(8,128)(2,1)} %bitcast.5, bf16[8,128,1152]{2,1,0:T(8,128)(2,1)} %bitcast.6, bf16[36,1728]{1,0:T(8,128)(2,1)} %w1_ref.1, ...), custom_call_target="tpu_custom_call" | custom-call | tf_op jit(solution)/shard_map/block/pallas_call | solution.py:613
  116.9 0.0 copy-start
  116.9 3.3 %copy.14 = bf16[1,8,128,1152]{3,2,1,0:T(8,128)(2,1)} copy(bf16[1,8,128,1152]{3,2,1,0:T(8,128)(2,1)} %bitcast.7) | data formatting | bytes 4718592
  120.2 0.0 copy-done
  120.2 0.6 copy.15
Async XLA Ops:
  116.9 3.3 %copy-start = (f32[36,72]{1,0:T(8,128)S(1)}, f32[36,72]{1,0:T(8,128)}, u32[]{:S(2)}) copy-start(f32[36,72]{1,0:T(8,128)} %get-tuple-element.9) | copy-start | bytes 31108

commit v8 on v7

--- a/solution.py
+++ b/solution.py
@@ -75,12 +75,12 @@
     (("upq0", "dnq0"), ("farq0",)),
     (("upp1", "dnp1"), ("farp1",)),
     (("upq1", "dnq1"), ("farq1",)),
-    (("farp0", "farq0"), ("s0",)),
     (("upp2", "dnp2"), ("farp2",)),
     (("upq2", "dnq2"), ("farq2",)),
-    (("farp1", "farq1"), ("s1",)),
     (("upp3", "dnp3"), ("farp3",)),
     (("upq3", "dnq3"), ("farq3",)),
+    (("farp0", "farq0"), ("s0",)),
+    (("farp1", "farq1"), ("s1",)),
     (("farp2", "farq2"), ("s2",)),
     (("farp3", "farq3"), ("s3",)),
 )
@@ -369,7 +369,7 @@
         for n in range(batches):
             @pl.when(i == n)
             def _(n=n):
-                for run in steps_t[(9, 12, 12, 15)[n] : (12, 12, 15, 15)[n]]:
+                for run in steps_t[(9, 11, 13, 13)[n] : (11, 13, 13, 13)[n]]:
                     run()
 
     loads[1].wait()
@@ -383,7 +383,7 @@
         for n in range(batches):
             @pl.when(i == n)
             def _(n=n):
-                for run in steps_t[(15, 18, 19, 19)[n] : (18, 19, 19, 19)[n]]:
+                for run in steps_t[(13, 15, 17, 18)[n] : (15, 17, 18, 19)[n]]:
                     run()
 
         @pl.when(busy)

time: 121 us -> 114 us (0.942)
  Pallas kernels: 116 us -> 108 us
    pallas_call x1, Pallas kernels: 116 us -> 108 us  [on_device(): pl.pallas_call(block_kernel, out_shape=(jax.ShapeDtypeStruct(frames, BF),...]
where the time goes in v8:
time: 114 us; the launch traced here: 113 us
  Pallas kernels  108 us (95%)
  local copies, waits for them, and re-layouts  3.88 us (3%)
  between operations  1.3 us (1%)
    pallas_call x1, Pallas kernels, on_device(): pl.pallas_call(block_kernel, out_shape=(jax.ShapeDtypeStruct(frames, BF),...  108 us
    unnamed x4, local copies, waits for them, and re-layouts  3.88 us

profile of v8, /device:TPU:7, one launch (start us, length us, event | category | flops | bytes accessed | tf_op | source)
XLA Modules:
  0.0 113.5 jit_solution(6980222802249948586)
XLA Ops:
  1.3 108.3 %block.1 = (bf16[8,128,1152]{2,1,0:T(8,128)(2,1)}, f32[36,72]{1,0:T(8,128)}) custom-call(s32[1]{0:T(128)S(6)} %copy.13.total_ref, f32[4,1152]{1,0:T(4,128)} %bitcast.8, f32[2,1152]{1,0:T(2,128)} %bitcast.9, bf16[8,128,1152]{2,1,0:T(8,128)(2,1)} %bitcast.5, bf16[8,128,1152]{2,1,0:T(8,128)(2,1)} %bitcast.6, bf16[36,1728]{1,0:T(8,128)(2,1)} %w1_ref.1, ...), custom_call_target="tpu_custom_call" | custom-call | tf_op jit(solution)/shard_map/block/pallas_call | solution.py:613
  109.6 0.0 copy-start
  109.6 3.3 %copy.14 = bf16[1,8,128,1152]{3,2,1,0:T(8,128)(2,1)} copy(bf16[1,8,128,1152]{3,2,1,0:T(8,128)(2,1)} %bitcast.7) | data formatting | bytes 4718592
  112.9 0.0 copy-done
  112.9 0.6 copy.15
Async XLA Ops:
  109.6 3.3 %copy-start = (f32[36,72]{1,0:T(8,128)S(1)}, f32[36,72]{1,0:T(8,128)}, u32[]{:S(2)}) copy-start(f32[36,72]{1,0:T(8,128)} %get-tuple-element.9) | copy-start | bytes 31108
